TPU v7x, 128 devices: a whole 4x4x4 slice. The times are simulated.
128 devices in a mesh: radon: 8 (over y_lo, z), freq: 16 (over y_hi, x, core).
Axes of the slice: x: 4, y: 4 (y_hi: 2, y_lo: 2; y = y_hi * 2 + y_lo), z: 4, core: 2. Of those that a mesh axis runs over, the one named last changes fastest.
Arguments:
- shot_traces: float32 [384, 1024, 1024], P('radon', 'freq'), may hold values from -6 to 6
- radon_weights: float32 [2, 1024, 256], P(None, 'freq'), may hold values from -0.1875 to 0.1875
- source_weights: float32 [384, 256], replicated, may hold values from -0.01953125 to 0.01953125
- line_index: int32 [384], replicated, may hold values from 0 to 1, as said below
- panel_index: int32 [384], replicated, may hold values from 0 to 1, as said below
Outputs:
- multiples: float32 [256, 2, 384, 256], P('freq', None, 'radon')
Inputs may be any that keep to these rules, and one draw needn't show every extreme that they name: `line_index`: in every aligned block of 48 shots, each geometry holds exactly 24 shots. `panel_index`: in every aligned block of 48 shots, each panel holds exactly 24 shots.
All inputs are finite; a program needn't handle non-finite values.
Results may differ from a plain program's by a relative error of at most 0.0001.
Values sent between devices are 32-bit elements; how exact they have to be, the bound alone decides.
No kernel may reach another device: no remote copies, remote signals or barrier semaphores. Data moves between devices by JAX's collectives and lax.ppermute only.
A program may use at most 128 MiB of HBM per device.

v0:
```python
import math

import jax
import jax.numpy as jnp
from jax import lax
from jax.sharding import PartitionSpec as P

NT = 1024
NF = 256
P_SIZE = 256
L = 2
K = 2


highest = lax.Precision.HIGHEST


def dft_tables(bin_count, samples):
    bins = jnp.arange(bin_count, dtype=jnp.int32)
    ticks = jnp.arange(samples, dtype=jnp.int32)
    phase = (ticks[:, None] * bins[None, :] % samples).astype(jnp.float32) * (
        2.0 * math.pi / samples
    )
    factor = samples ** (-0.5)
    return (jnp.cos(phase) * factor, -jnp.sin(phase) * factor)


def shards(shot_traces, radon_weights, source_weights, line_index, panel_index):
    shot_rows = shot_traces.shape[0]
    offset = lax.axis_index("radon") * shot_rows
    own_lines = lax.dynamic_slice_in_dim(line_index, offset, shot_rows)
    own_ids = lax.dynamic_slice_in_dim(panel_index, offset, shot_rows)
    band_rows = NF // lax.axis_size("freq")
    line_onehot = (own_lines[:, None] == jnp.arange(L, dtype=jnp.int32)[None, :]).astype(
        jnp.float32
    )
    selected = jnp.einsum("sl,lxp->sxp", line_onehot, radon_weights, precision=highest)
    cosines, sines = dft_tables(band_rows * lax.axis_size("freq"), NT)
    real_part = jnp.einsum("sxt,tf->sxf", shot_traces, cosines, precision=highest)
    imag_part = jnp.einsum("sxt,tf->sxf", shot_traces, sines, precision=highest)
    gathers = lax.psum_scatter(
        jnp.stack(
            [
                jnp.einsum("sxp,sxf->fsp", selected, real_part, precision=highest),
                jnp.einsum("sxp,sxf->fsp", selected, imag_part, precision=highest),
            ],
            axis=1,
        ),
        "freq",
        scatter_dimension=0,
        tiled=True,
    )
    own_real = gathers[:, 0]
    own_imag = gathers[:, 1]
    block_rows = lax.all_gather(gathers, "radon", axis=2, tiled=True)
    row_count = block_rows.shape[2]
    block_order = jnp.argsort(panel_index, stable=True)
    sorted_weights = jnp.take(source_weights, block_order, axis=0).reshape(
        K, row_count // K, P_SIZE
    )
    sorted_rows = jnp.take(block_rows, block_order, axis=2)
    sorted_rows = sorted_rows.reshape(sorted_rows.shape[0], 2, K, row_count // K, P_SIZE)
    panels = jnp.einsum("kmq,fckmp->kfcqp", sorted_weights, sorted_rows, precision=highest)
    panel_real = panels[:, :, 0]
    panel_imag = panels[:, :, 1]
    own_order = jnp.argsort(own_ids, stable=True)
    own_back = jnp.argsort(own_order, stable=True)
    group_real = jnp.take(own_real, own_order, axis=1).reshape(band_rows, K, shot_rows // K, P_SIZE)
    group_imag = jnp.take(own_imag, own_order, axis=1).reshape(band_rows, K, shot_rows // K, P_SIZE)
    real_part = jnp.einsum(
        "fkmq,kfqp->fkmp", group_real, panel_real, precision=highest
    ) - jnp.einsum("fkmq,kfqp->fkmp", group_imag, panel_imag, precision=highest)
    imag_part = jnp.einsum(
        "fkmq,kfqp->fkmp", group_real, panel_imag, precision=highest
    ) + jnp.einsum("fkmq,kfqp->fkmp", group_imag, panel_real, precision=highest)
    result_real = jnp.take(real_part.reshape(band_rows, shot_rows, P_SIZE), own_back, axis=1)
    result_imag = jnp.take(imag_part.reshape(band_rows, shot_rows, P_SIZE), own_back, axis=1)
    multiples = jnp.stack([result_real, result_imag], axis=1)
    return multiples


def solution(mesh):
    placed = (P("radon", "freq", None), P(None, "freq", None), P(), P(), P())
    return jax.shard_map(
        shards,
        mesh=mesh,
        in_specs=placed,
        out_specs=P("freq", None, "radon", None),
        check_vma=False,
    )
```

profile of v0, /device:TPU:1, one launch (start us, length us, event | category | flops | bytes accessed | tf_op | source)
XLA Modules:
  0.0 509.8 jit_solution(15867928366108315933)
XLA Ops:
  6.5 18.2 %fusion.27 = f32[256,48,64]{0,2,1:T(8,128)} fusion(f32[48,64,1024]{2,1,0:T(8,128)} %param.7), kind=kOutput, calls=%fused_computation.39 | convolution fusion | flops 9667608576 | bytes 15728640 | tf_op jit(solution)/shard_map/sxt,tf->sxf/dot_general | solution.py:39
  24.8 18.7 %fusion.25 = f32[256,48,64]{0,2,1:T(8,128)S(1)} fusion(f32[48,64,1024]{2,1,0:T(8,128)S(1)} %copy-done.3), kind=kOutput, calls=%fused_computation.37 | convolution fusion | flops 9667870720 | bytes 15728640 | tf_op jit(solution)/shard_map/sxt,tf->sxf/dot_general | solution.py:40
  44.3 2.4 fusion.49
  46.7 14.9 %convolution_bitcast_fusion.1 = f32[256,1,48,256]{3,0,2,1:T(8,128)S(1)} fusion(f32[256,48,64]{0,2,1:T(8,128)} %fusion.27, f32[48,64,256]{2,0,1:T(8,128)S(1)} %fusion.49), kind=kOutput, calls=%fused_computation.23 | convolution fusion | flops 2415919104 | bytes 18874368 | tf_op jit(solution)/shard_map/sxp,sxf->fsp/dot_general | solution.py:44
  61.6 12.9 %convolution_bitcast_fusion = f32[256,1,48,256]{3,0,2,1:T(8,128)S(1)} fusion(f32[256,48,64]{0,2,1:T(8,128)S(1)} %fusion.25, f32[48,64,256]{2,0,1:T(8,128)S(1)} %fusion.49), kind=kOutput, calls=%fused_computation.22 | convolution fusion | flops 2415919104 | bytes 18874368 | tf_op jit(solution)/shard_map/sxp,sxf->fsp/dot_general | solution.py:45
  74.5 9.3 %pad_maximum_fusion = f32[256,2,48,256]{3,0,2,1:T(8,128)} fusion(f32[256,1,48,256]{3,0,2,1:T(8,128)S(1)} %convolution_bitcast_fusion, f32[256,1,48,256]{3,0,2,1:T(8,128)S(1)} %convolution_bitcast_fusion.1), kind=kLoop, calls=%fused_computation.6 | loop fusion | flops 6291456 | bytes 50331648 | tf_op jit(solution)/shard_map/stack | solution.py:42
  83.9 193.3 %reduce-scatter.2.cloned.1.call-done = f32[16,2,48,256]{3,0,2,1:T(8,128)} async-done(((f32[256,2,48,256]{3,0,2,1:T(8,128)}), f32[16,2,48,256]{3,0,2,1:T(8,128)}) %reduce-scatter.2.cloned.1.call-update) | async-done | bytes 1572880 | tf_op jit(solution)/shard_map/reduce_scatter | solution.py:41
  277.3 3.8 sort.49
  281.2 2.0 sort.48
  283.2 1.7 gather_fusion.1
  284.9 2.0 sort.50
  287.0 1.7 slice_bitcast_fusion.2
  288.7 1.5 gather_fusion.2
  290.2 1.5 gather_fusion.3
  291.7 1.5 broadcast_select_fusion
  293.2 114.5 %all-gather.2.cloned.1.call-done = f32[16,2,384,256]{3,0,2,1:T(8,128)} async-done(((f32[16,2,48,256]{3,0,2,1:T(8,128)}), f32[16,2,384,256]{3,0,2,1:T(8,128)}) %all-gather.2.cloned.1.call-update) | async-done | bytes 12582928 | tf_op jit(solution)/shard_map/all_gather | solution.py:55
  407.8 10.4 %gather_fusion = f32[384,16,2,256]{3,1,2,0:T(8,128)} fusion(f32[16,2,384,256]{3,0,2,1:T(8,128)} %all-gather.2.cloned.1.call-done, s32[1024]{0:T(1024)S(1)} %pad_clamp_fusion.1), kind=kCustom, calls=%fused_computation.4 | custom fusion | bytes 25167360 | tf_op jit(solution)/shard_map/jit(_take)/gather | solution.py:61
  418.2 41.1 %fusion.9 = f32[2,16,2,256,256]{3,4,2,1,0:T(8,128)S(1)} fusion(f32[16,2,2,192,256]{4,0,1,3,2:T(8,128)} %bitcast.60, pred[2,192]{1,0:T(4,128)(4,1)S(1)} %broadcast_in_dim.37, f32[2,192,256]{2,1,0:T(8,128)S(1)} %bitcast.69), kind=kOutput, calls=%fused_computation.19 | convolution fusion | flops 9666920448 | bytes 29753728 | tf_op jit(solution)/shard_map/kmq,fckmp->kfcqp/dot_general | solution.py:63
  459.2 6.7 %slice_bitcast_fusion.1 = (f32[2,16,256,256]{2,3,1,0:T(8,128)}, f32[2,16,256,256]{2,3,1,0:T(8,128)}) fusion(f32[2,16,2,256,256]{3,4,2,1,0:T(8,128)S(1)} %fusion.9), kind=kLoop, calls=%fused_computation.10 | loop fusion | bytes 33554432 | tf_op jit(solution)/shard_map/squeeze | solution.py:64
  465.9 9.6 %fusion.1 = f32[16,2,24,256]{3,2,1,0:T(8,128)S(1)} fusion(f32[2,16,256,256]{2,3,1,0:T(8,128)} %get-tuple-element.13, f32[16,2,24,256]{3,0,2,1:T(8,128)S(1)} %bitcast.63), kind=kOutput, calls=%fused_computation.11 | convolution fusion | flops 603979776 | bytes 9961472 | tf_op jit(solution)/shard_map/fkmq,kfqp->fkmp/dot_general | solution.py:73
  475.6 7.4 %fusion.3 = f32[16,2,24,256]{3,2,1,0:T(8,128)S(1)} fusion(f32[2,16,256,256]{2,3,1,0:T(8,128)S(1)} %copy-done.2, f32[16,2,24,256]{3,0,2,1:T(8,128)S(1)} %bitcast.65), kind=kOutput, calls=%fused_computation.13 | convolution fusion | flops 603979776 | bytes 9961472 | tf_op jit(solution)/shard_map/fkmq,kfqp->fkmp/dot_general | solution.py:72
  483.1 7.7 %fusion.19 = f32[16,2,24,256]{3,2,1,0:T(8,128)S(1)} fusion(f32[16,2,24,256]{3,2,1,0:T(8,128)S(1)} %fusion.1, f32[2,16,256,256]{2,3,1,0:T(8,128)S(1)} %bitcast.62, f32[16,2,24,256]{3,0,2,1:T(8,128)S(1)} %bitcast.66), kind=kOutput, calls=%fused_computation.33 | convolution fusion | flops 604176384 | bytes 10747904 | tf_op jit(solution)/shard_map/fkmq,kfqp->fkmp/dot_general | solution.py:75
  491.2 7.5 %fusion.16 = f32[16,2,24,256]{3,2,1,0:T(8,128)S(1)} fusion(f32[16,2,24,256]{3,2,1,0:T(8,128)S(1)} %fusion.3, f32[2,16,256,256]{2,3,1,0:T(8,128)S(1)} %bitcast.62, f32[16,2,24,256]{3,0,2,1:T(8,128)S(1)} %bitcast.64), kind=kOutput, calls=%fused_computation.32 | convolution fusion | flops 604176384 | bytes 10747904 | tf_op jit(solution)/shard_map/fkmq,kfqp->fkmp/dot_general | solution.py:70
  500.7 2.1 copy.32
  (40 shorter events, 3.6 us)
Async XLA Ops:
  6.5 276.7 %copy-start = (f32[384,256]{1,0:T(8,128)S(1)}, f32[384,256]{1,0:T(8,128)}, u32[]{:S(2)}) copy-start(f32[384,256]{1,0:T(8,128)} %param.9) | copy-start | bytes 1179652
  6.5 270.6 %reduce-scatter.2.cloned.1.call-start = ((), (), s32[]{:S(2)}) async-start(), calls=%async_computation.1 | async-start | bytes 26738688 | tf_op jit(solution)/shard_map/reduce_scatter | solution.py:41
  6.5 18.2 %copy-start.3 = (f32[48,64,1024]{2,1,0:T(8,128)S(1)}, f32[48,64,1024]{2,1,0:T(8,128)}, u32[]{:S(2)}) copy-start(f32[48,64,1024]{2,1,0:T(8,128)} %param.7) | copy-start | bytes 37748740
  83.8 193.4 %copy-start.4 = (s32[384]{0:T(512)S(1)}, s32[384]{0:T(512)}, u32[]{:S(2)}) copy-start(s32[384]{0:T(512)} %param.11) | copy-start | bytes 4612
  83.8 323.9 %all-gather.2.cloned.1.call-start = ((), (), s32[]{:S(2)}) async-start(), calls=%async_computation.2 | async-start | bytes 14155776 | tf_op jit(solution)/shard_map/all_gather | solution.py:55
  465.9 9.7 %copy-start.2 = (f32[2,16,256,256]{2,3,1,0:T(8,128)S(1)}, f32[2,16,256,256]{2,3,1,0:T(8,128)}, u32[]{:S(2)}) copy-start(f32[2,16,256,256]{2,3,1,0:T(8,128)} %get-tuple-element.13) | copy-start | bytes 25165828
  465.9 17.1 %slice-start = ((s8[8388608]{0:T(1024)(128)(4,1)}), s8[4194304]{0:T(1024)(128)(4,1)S(1)}, s32[]{:S(2)}) async-start(s8[8388608]{0:T(1024)(128)(4,1)} %bitcast.61), calls=%async_computation.3 | async-start | bytes 8388608
  475.6 7.5 %slice-start.1 = ((s8[8388608]{0:T(1024)(128)(4,1)}), s8[4194304]{0:T(1024)(128)(4,1)S(1)}, s32[]{:S(2)}) async-start(s8[8388608]{0:T(1024)(128)(4,1)} %bitcast.61), calls=%async_computation.4 | async-start | bytes 8388608
  491.2 11.5 %copy-start.1 = (f32[384,256]{1,0:T(8,128)S(1)}, f32[384,256]{1,0:T(8,128)}, u32[]{:S(2)}) copy-start(f32[384,256]{1,0:T(8,128)} %param.9) | copy-start | bytes 1179652
Sparse Core Ops, SparseCore 0:
  83.9 193.1 reduce-scatter.1
  278.9 128.7 all-gather.1
where the time goes:
time: 514 us; the launch traced here: 510 us
  waiting for transfers between devices  308 us (60%)
  matrix products  140 us (27%)
  local copies, waits for them, and re-layouts  28.6 us (6%)
  other arithmetic  19 us (4%)
  between operations  13.8 us (3%)
    reduce_scatter x1, waiting for transfers between devices, shards(): lax.psum_scatter(jnp.stack([jnp.einsum('sxp,sxf->fsp', selected, real_par...  193 us
    all_gather x1, waiting for transfers between devices, shards(): block_rows = lax.all_gather(gathers, 'radon', axis=2, tiled=True)  115 us
    dot_general x1, matrix products, shards(): jnp.einsum('kmq,fckmp->kfcqp', sorted_weights, sorted_rows, precision=hig...  41.1 us
    dot_general x1, matrix products, shards(): imag_part = jnp.einsum('sxt,tf->sxf', shot_traces, sines, precision=highest)  18.7 us
    dot_general x1, matrix products, shards(): jnp.einsum('sxt,tf->sxf', shot_traces, cosines, precision=highest)  18.2 us
    dot_general x1, matrix products, shards(): jnp.einsum('sxp,sxf->fsp', selected, real_part, precision=highest)  14.9 us
    dot_general x1, matrix products, shards(): jnp.einsum('sxp,sxf->fsp', selected, imag_part, precision=highest)  12.9 us
    gather x1, local copies, waits for them, and re-layouts, shards(): sorted_rows = jnp.take(block_rows, block_order, axis=2)  10.4 us
  transfers between devices with their start and end apart: 2, of which 2 were waited for; matrix products, arithmetic and copies ran while one was open for 3% of the time, Pallas kernels for 0%

commit v1 on v0

v1 whole, which is shorter than its diff:
```python
import functools

import jax
import jax.numpy as jnp
import ml_dtypes
import numpy as np
from jax import lax
from jax.experimental import pallas as pl
from jax.experimental.pallas import tpu as pltpu
from jax.sharding import PartitionSpec as P

NT = 1024
NF = 256
P_SIZE = 256
L = 2
K = 2
HALF = NT // 2
LANES = 128
BINS = 2
ROWS = 8
SPREAD = ROWS // (2 * BINS)


def split(x):
    hi = x.astype(jnp.bfloat16)
    lo = (x - hi.astype(jnp.float32)).astype(jnp.bfloat16)
    return hi, lo


def dot3(a, b, dims=(((1,), (0,)), ((), ()))):
    dot = functools.partial(
        lax.dot_general, dimension_numbers=dims, preferred_element_type=jnp.float32
    )
    return dot(a[0], b[0]) + (dot(a[0], b[1]) + dot(a[1], b[0]))


def dft_tables(radon_size, freq_size):
    band = NF // freq_size
    device = np.arange(radon_size * freq_size)
    rows = []
    for parity in range(BINS):
        bins = band * (device % freq_size) + BINS * (device // freq_size) + parity
        phase = (bins[:, None] * np.arange(HALF)[None, :] % NT) * (2.0 * np.pi / NT)
        rows += [np.cos(phase), -np.sin(phase)]
    table = (np.concatenate(rows) * NT ** (-0.5)).astype(np.float32)
    hi = table.astype(ml_dtypes.bfloat16)
    lo = (table - hi.astype(np.float32)).astype(ml_dtypes.bfloat16)
    return np.stack([hi, lo])


def dft_kernel(devices, *refs):
    count = 4 * SPREAD
    x_refs, (table_ref, out_ref), tiles = refs[:count], refs[count : count + 2], refs[count + 2 :]
    for sh in range(SPREAD):
        rows = jnp.concatenate([x_refs[SPREAD * i + sh][0] for i in range(4)], axis=0)
        head, tail = rows[:, :HALF], rows[:, HALF:]
        for parity in range(BINS):
            folded = split(head - tail if parity else head + tail)
            at = slice(2 * parity * devices, 2 * (parity + 1) * devices)
            spectrum = dot3(
                (table_ref[0, at], table_ref[1, at]), folded, (((1,), (1,)), ((), ()))
            )
            for part in range(2):
                row = (sh * BINS + parity) * 2 + part
                for h, tile in enumerate(tiles):
                    tile[pl.ds(row, devices, stride=ROWS), :] = spectrum[
                        part * devices : (part + 1) * devices, h * LANES : (h + 1) * LANES
                    ]
    for h, tile in enumerate(tiles):
        out_ref[:, h * LANES : (h + 1) * LANES] = tile[...]


def dft(traces, radon_size, freq_size):
    shots, channels, _ = traces.shape
    devices = radon_size * freq_size
    step = 4 * SPREAD
    lanes = shots // SPREAD * channels
    table = jnp.asarray(dft_tables(radon_size, freq_size))
    return pl.pallas_call(
        functools.partial(dft_kernel, devices),
        grid=(shots // step,),
        in_specs=[
            pl.BlockSpec((1, channels, NT), lambda g, n=n: (g * step + n, 0, 0))
            for n in range(step)
        ]
        + [pl.BlockSpec(table.shape, lambda g: (0, 0, 0))],
        out_specs=pl.BlockSpec((devices * ROWS, 4 * channels), lambda g: (0, g)),
        out_shape=jax.ShapeDtypeStruct((devices * ROWS, lanes), jnp.float32),
        scratch_shapes=[pltpu.VMEM((devices * ROWS, LANES), jnp.float32)]
        * (4 * channels // LANES),
        compiler_params=pltpu.CompilerParams(vmem_limit_bytes=48 * 2**20),
        cost_estimate=pl.CostEstimate(
            flops=3 * table.size * shots * channels,
            bytes_accessed=4 * (traces.size + devices * ROWS * lanes),
            transcendentals=0,
        ),
    )(*[traces] * step, table)


def weights_kernel(w_ref, hi_ref, lo_ref):
    channels = w_ref.shape[2]
    for j in range(w_ref.shape[0]):
        for line in range(L):
            at = (pl.ds(j * channels, channels), pl.ds(line * P_SIZE, P_SIZE))
            hi_ref[at], lo_ref[at] = split(w_ref[j, line])


def split_weights(weights):
    freq_size, _, channels, _ = weights.shape
    out = jax.ShapeDtypeStruct((freq_size * channels, L * P_SIZE), jnp.bfloat16)
    return pl.pallas_call(
        weights_kernel,
        out_shape=(out, out),
        compiler_params=pltpu.CompilerParams(vmem_limit_bytes=48 * 2**20),
        cost_estimate=pl.CostEstimate(
            flops=10**11, bytes_accessed=8 * weights.size, transcendentals=0
        ),
    )(weights)


def panel_kernel(freq_size, count, *refs):
    rec_refs = refs[:count]
    (hi_ref, lo_ref, line_ref, src_ref, panel_ref, out_ref, a_hi, a_lo) = refs[count : count + 8]
    gathers = refs[count + 8 :]
    step = pl.program_id(0)
    steps = pl.num_programs(0)
    channels = hi_ref.shape[0] // freq_size
    slots = rec_refs[0].shape[1] // channels

    low = lax.broadcasted_iota(jnp.int32, (ROWS, 2 * channels), 1) < channels
    for r, rec_ref in enumerate(rec_refs):
        for t in range(slots // 2):
            firsts, seconds = [], []
            for pair in range(freq_size // 2):
                at = pl.ds(t * 2 * channels, 2 * channels)
                a = rec_ref[pl.ds(2 * pair * ROWS, ROWS), at]
                b = rec_ref[pl.ds((2 * pair + 1) * ROWS, ROWS), at]
                firsts.append(jnp.where(low, a, pltpu.roll(b, channels, 1)))
                seconds.append(jnp.where(low, pltpu.roll(a, channels, 1), b))
            both = jnp.concatenate(
                [jnp.concatenate(firsts, axis=1), jnp.concatenate(seconds, axis=1)], axis=0
            )
            at = pl.ds((r * slots + 2 * t) * ROWS, 2 * ROWS)
            a_hi[at, :], a_lo[at, :] = split(both)
    lines = dot3((a_hi[...], a_lo[...]), (hi_ref[...], lo_ref[...]))
    rows = count * slots * ROWS
    chosen = jnp.where(line_ref[...] == 0, lines[:, :P_SIZE], lines[:, P_SIZE:])
    for h, tile in enumerate(gathers):
        tile[pl.ds(pl.multiple_of(step * rows, rows), rows), :] = chosen[
            :, h * LANES : (h + 1) * LANES
        ]

    @pl.when(step == steps - 1)
    def _():
        shots = src_ref.shape[1]
        own = shots // out_ref.shape[0]
        source = split(src_ref[...])
        first = panel_ref[...] == 0
        for n in range(BINS):
            parts, panels = [], []
            for part in range(2):
                at = pl.ds(2 * n + part, shots, stride=2 * BINS)
                rows = jnp.concatenate([tile[at, :] for tile in gathers], axis=1)
                parts.append(split(rows))
                panels.append(dot3(source, parts[part]))
            chosen = None
            for k in range(K):
                at = slice(k * P_SIZE, (k + 1) * P_SIZE)
                real, imag = split(panels[0][at]), split(panels[1][at])
                out_real = dot3(parts[0], real) - dot3(parts[1], imag)
                out_imag = dot3(parts[0], imag) + dot3(parts[1], real)
                if k == 0:
                    chosen = (out_real, out_imag)
                else:
                    chosen = (
                        jnp.where(first, chosen[0], out_real),
                        jnp.where(first, chosen[1], out_imag),
                    )
            for part in range(2):
                for r in range(out_ref.shape[0]):
                    out_ref[r, n, part] = chosen[part][r * own : (r + 1) * own]


def panel_products(received, weights, lines, sources, panel_rows, freq_size, radon_size):
    lanes = received.shape[1]
    depth, columns = weights[0].shape
    channels = depth // freq_size
    slots = lanes // channels
    grid = 4
    count = radon_size // grid
    rows = count * slots * ROWS
    shots = sources.shape[1]
    out = (radon_size, BINS, 2, shots // radon_size, P_SIZE)
    return pl.pallas_call(
        functools.partial(panel_kernel, freq_size, count),
        grid=(grid,),
        in_specs=[
            pl.BlockSpec((freq_size * ROWS, lanes), lambda r, n=n: (count * r + n, 0))
            for n in range(count)
        ]
        + [
            pl.BlockSpec((depth, columns), lambda r: (0, 0)),
            pl.BlockSpec((depth, columns), lambda r: (0, 0)),
            pl.BlockSpec((rows, 1), lambda r: (r, 0)),
            pl.BlockSpec(sources.shape, lambda r: (0, 0)),
            pl.BlockSpec((shots, 1), lambda r: (0, 0)),
        ],
        out_specs=pl.BlockSpec(out, lambda r: (0, 0, 0, 0, 0)),
        out_shape=jax.ShapeDtypeStruct(out, jnp.float32),
        scratch_shapes=[pltpu.VMEM((rows, depth), jnp.bfloat16)] * 2
        + [pltpu.VMEM((grid * rows, LANES), jnp.float32)] * (P_SIZE // LANES),
        compiler_params=pltpu.CompilerParams(vmem_limit_bytes=48 * 2**20),
        cost_estimate=pl.CostEstimate(
            flops=6 * grid * rows * depth * columns,
            bytes_accessed=4 * received.size,
            transcendentals=0,
        ),
    )(*[received] * count, *weights, lines, sources, panel_rows)


def shards(shot_traces, radon_weights, source_weights, line_index, panel_index):
    shot_rows = shot_traces.shape[0]
    freq_size = lax.axis_size("freq")
    radon_size = lax.axis_size("radon")

    weights = lax.all_gather(radon_weights, "freq", axis=0)
    weights = split_weights(weights)
    messages = dft(shot_traces, radon_size, freq_size)
    received = lax.all_to_all(messages, ("radon", "freq"), 0, 0, tiled=True)

    lines = jnp.repeat(line_index, 2 * BINS)[:, None]
    onehot = panel_index[None, :] == jnp.arange(K, dtype=jnp.int32)[:, None]
    sources = jnp.where(onehot[:, None, :], source_weights.T[None], 0.0).reshape(K * P_SIZE, -1)

    products = panel_products(
        received, weights, lines, sources, panel_index[:, None], freq_size, radon_size
    )
    result = lax.all_to_all(products, "radon", 0, 0, tiled=True)
    return result.reshape(BINS * radon_size, 2, shot_rows, P_SIZE)


def solution(mesh):
    placed = (P("radon", "freq", None), P(None, "freq", None), P(), P(), P())
    return jax.shard_map(
        shards,
        mesh=mesh,
        in_specs=placed,
        out_specs=P("freq", None, "radon", None),
        check_vma=False,
    )
```

time: 514 us -> 162 us (0.32)
  waiting for transfers between devices: 308 us -> 78.3 us
  matrix products: 140 us -> 0 us
  blocking collectives: 0 us -> 27.3 us
  Pallas kernels: 0 us -> 23.5 us
  local copies, waits for them, and re-layouts: 28.6 us -> 6.75 us
  other arithmetic: 19 us -> 0.06 us
  starting transfers between devices: 0.04 us -> 11.9 us
    reduce_scatter x1 -> x0, waiting for transfers between devices: 193 us -> none  [shards(): lax.psum_scatter(jnp.stack([jnp.einsum('sxp,sxf->fsp', selected, real_par...]
    dot_general x10 -> x0, matrix products: 140 us -> none  [the longest x1 41.1 us: shards(): jnp.einsum('kmq,fckmp->kfcqp', sorted_weights, sorted_rows, precision=hig...]
    all_gather x1, waiting for transfers between devices: 115 us -> 77.6 us  [shards(): weights = lax.all_gather(radon_weights, 'freq', axis=0)]
    all_to_all x0 -> x1, blocking collectives: none -> 27.3 us  [shards(): result = lax.all_to_all(products, 'radon', 0, 0, tiled=True)]
    pallas_call x0 -> x3, Pallas kernels: none -> 23.5 us  [the longest x1 11.9 us: panel_products(): pl.pallas_call(functools.partial(panel_kernel, freq_size, count), grid=(g...]
    gather x6 -> x0, local copies, waits for them, and re-layouts: 16.3 us -> none  [the longest x1 10.4 us: shards(): sorted_rows = jnp.take(block_rows, block_order, axis=2)]
    all_to_all x0 -> x1, starting transfers between devices: none -> 11.9 us  [shards(): received = lax.all_to_all(messages, ('radon', 'freq'), 0, 0, tiled=True)]
    another operation x3 -> x0, other arithmetic: 9.56 us -> none  [the longest x1 9.26 us: shards(): jnp.stack([jnp.einsum('sxp,sxf->fsp', selected, real_part, precision=high...]
  transfers between devices with their start and end apart: 2 -> 2, of which waited for: 2 -> 1; matrix products, arithmetic and copies ran while one was open for 3% -> 0% of each run, Pallas kernels for 0% -> 7%
where the time goes in v1:
time: 162 us; the launch traced here: 161 us
  waiting for transfers between devices  78.3 us (48%)
  blocking collectives  27.3 us (17%)
  Pallas kernels  23.5 us (15%)
  between operations  13.5 us (8%)
  starting transfers between devices  11.9 us (7%)
  local copies, waits for them, and re-layouts  6.75 us (4%)
    all_gather x1, waiting for transfers between devices, shards(): weights = lax.all_gather(radon_weights, 'freq', axis=0)  77.6 us
    all_to_all x1, blocking collectives, shards(): result = lax.all_to_all(products, 'radon', 0, 0, tiled=True)  27.3 us
    all_to_all x1, starting transfers between devices, shards(): received = lax.all_to_all(messages, ('radon', 'freq'), 0, 0, tiled=True)  11.9 us
    pallas_call x1, Pallas kernels, panel_products(): pl.pallas_call(functools.partial(panel_kernel, freq_size, count), grid=(g...  11.9 us
    pallas_call x1, Pallas kernels, dft(): pl.pallas_call(functools.partial(dft_kernel, devices), grid=(shots // ste...  11.3 us
    unnamed x15, local copies, waits for them, and re-layouts  6.16 us
  transfers between devices with their start and end apart: 2, of which 1 were waited for; matrix products, arithmetic and copies ran while one was open for 0% of the time, Pallas kernels for 7%

profile of v1, /device:TPU:1, one launch (start us, length us, event | category | flops | bytes accessed | tf_op | source)
XLA Modules:
  0.0 161.3 jit_solution(3239387978405480167)
XLA Ops:
  6.5 0.0 all-gather.3.cloned.1.call-start
  6.5 0.7 all-gather.3.cloned.1.call-update
  7.3 0.0 copy-start
  7.3 1.2 copy-done
  8.5 11.3 %shard_map.64 = f32[1024,1536]{1,0:T(8,128)} custom-call(f32[48,64,1024]{2,1,0:T(8,128)} %refs_7_.1, f32[48,64,1024]{2,1,0:T(8,128)} %refs_7_.1, f32[48,64,1024]{2,1,0:T(8,128)} %refs_7_.1, f32[48,64,1024]{2,1,0:T(8,128)} %refs_7_.1, f32[48,64,1024]{2,1,0:T(8,128)} %refs_7_.1, f32[48,64,1024]{2,1,0:T(8,128)} %refs_7_.1, f32[48,64,1024]{2,1,0:T(8,128)} %refs_7_.1, ...), custom_call_target="tpu_custom_call" | custom-call | flops 4831838208 | bytes 18874368 | tf_op jit(solution)/shard_map/pallas_call | solution.py:79
  19.8 0.0 copy-start.5
  19.8 11.9 %all-to-all-start = ((f32[128,8,1536]{2,1,0:T(8,128)}), f32[128,8,1536]{2,1,0:T(8,128)}, u32[]{:S(2)}, u32[]{:S(2)}) async-start(f32[128,8,1536]{2,1,0:T(8,128)} %bitcast.8), calls=%async_computation | async-start | bytes 12582912 | tf_op jit(solution)/shard_map/all_to_all | solution.py:229
  31.8 0.1 broadcast_in_dim.30
  31.9 0.2 broadcast_in_dim_reshape.4.refs_4_
  32.1 0.0 copy-done.4
  32.1 0.2 copy.11
  32.3 0.0 copy-done.5
  32.3 0.1 broadcast_in_dim.35.refs_6_
  32.4 0.1 broadcast_select_fusion
  32.5 77.6 %all-gather.3.cloned.1.call-done = f32[32,64,256]{2,1,0:T(8,128)} async-done(((f32[2,64,256]{2,1,0:T(8,128)}), f32[32,64,256]{2,1,0:T(8,128)}) %all-gather.3.cloned.1.call-update) | async-done | bytes 2097168 | tf_op jit(solution)/shard_map/all_gather | solution.py:226
  110.1 1.6 copy-done.3
  111.7 0.2 shard_map.65
  111.9 0.0 copy-start.1
  111.9 1.0 copy-done.1
  112.9 0.0 all-to-all-done
  112.9 1.2 copy-done.2
  114.1 11.9 %shard_map.66 = f32[8,2,2,48,256]{4,3,2,1,0:T(8,128)S(1)} custom-call(f32[1024,1536]{1,0:T(8,128)} %bitcast.1.refs_0_.refs_1_, f32[1024,1536]{1,0:T(8,128)} %bitcast.1.refs_0_.refs_1_, bf16[1024,512]{1,0:T(8,128)(2,1)S(1)} %get-tuple-element.7.refs_2_, bf16[1024,512]{1,0:T(8,128)(2,1)S(1)} %copy-done.2, s32[1536,1]{1,0:T(8,128)S(1)} %broadcast_in_dim_reshape.4.refs_4_, ...), custom_call_target="tpu_custom_call" | custom-call | flops 4831838208 | bytes 6291456 | tf_op jit(solution)/shard_map/pallas_call | solution.py:194
  126.0 27.3 %all_to_all.16 = f32[8,2,2,48,256]{4,3,2,1,0:T(8,128)S(1)} all-to-all(f32[8,2,2,48,256]{4,3,2,1,0:T(8,128)S(1)} %shard_map.66), channel_id=1, replica_groups=mesh['radon'=8,'freq'=16] {'radon'}, dimensions={0} | all-to-all | bytes 3145728 | tf_op jit(solution)/shard_map/all_to_all | solution.py:238
  153.3 1.1 copy.15
  (6 shorter events, 0.0 us)
Async XLA Ops:
  6.5 103.5 %all-gather.3.cloned.1.call-start = ((), (), s32[]{:S(2)}) async-start(), calls=%async_computation.2 | async-start | bytes 2228224 | tf_op jit(solution)/shard_map/all_gather | solution.py:226
  7.3 1.2 copy-start
  19.8 11.9 %copy-start.6 = (s32[384]{0:T(512)S(1)}, s32[384]{0:T(512)}, u32[]{:S(2)}) copy-start(s32[384]{0:T(512)} %param.9) | copy-start | bytes 4612
  19.8 12.3 %copy-start.4 = (f32[384,256]{1,0:T(8,128)S(1)}, f32[384,256]{1,0:T(8,128)}, u32[]{:S(2)}) copy-start(f32[384,256]{1,0:T(8,128)} %param.8) | copy-start | bytes 1179652
  19.8 12.5 %copy-start.5 = (s32[384]{0:T(512)S(1)}, s32[384]{0:T(512)}, u32[]{:S(2)}) copy-start(s32[384]{0:T(512)} %param.10) | copy-start | bytes 4612
  19.8 93.0 %all-to-all-start = ((f32[128,8,1536]{2,1,0:T(8,128)}), f32[128,8,1536]{2,1,0:T(8,128)}, u32[]{:S(2)}, u32[]{:S(2)}) async-start(f32[128,8,1536]{2,1,0:T(8,128)} %bitcast.8), calls=%async_computation | async-start | bytes 12582912 | tf_op jit(solution)/shard_map/all_to_all | solution.py:229
  110.1 1.6 copy-start.3
  111.9 1.0 copy-start.1
  112.9 1.2 copy-start.2
Sparse Core Ops, SparseCore 0:
  9.8 100.2 all-gather.2

commit v2 on v1

--- a/solution.py
+++ b/solution.py
@@ -49,10 +49,12 @@
 
 
 def dft_kernel(devices, *refs):
-    count = 4 * SPREAD
-    x_refs, (table_ref, out_ref), tiles = refs[:count], refs[count : count + 2], refs[count + 2 :]
+    x_refs, (table_ref, out_ref) = refs[:-2], refs[-2:]
+    groups = len(x_refs) // SPREAD
+    width = groups * x_refs[0].shape[1] // LANES
+    message = out_ref.shape[0] // devices
     for sh in range(SPREAD):
-        rows = jnp.concatenate([x_refs[SPREAD * i + sh][0] for i in range(4)], axis=0)
+        rows = jnp.concatenate([x_refs[SPREAD * i + sh][0] for i in range(groups)], axis=0)
         head, tail = rows[:, :HALF], rows[:, HALF:]
         for parity in range(BINS):
             folded = split(head - tail if parity else head + tail)
@@ -61,20 +63,19 @@
                 (table_ref[0, at], table_ref[1, at]), folded, (((1,), (1,)), ((), ()))
             )
             for part in range(2):
-                row = (sh * BINS + parity) * 2 + part
-                for h, tile in enumerate(tiles):
-                    tile[pl.ds(row, devices, stride=ROWS), :] = spectrum[
+                for h in range(width):
+                    tile = pl.program_id(0) * width + h
+                    row = tile * ROWS + (sh * BINS + parity) * 2 + part
+                    out_ref[pl.ds(row, devices, stride=message), :] = spectrum[
                         part * devices : (part + 1) * devices, h * LANES : (h + 1) * LANES
                     ]
-    for h, tile in enumerate(tiles):
-        out_ref[:, h * LANES : (h + 1) * LANES] = tile[...]
 
 
 def dft(traces, radon_size, freq_size):
     shots, channels, _ = traces.shape
     devices = radon_size * freq_size
     step = 4 * SPREAD
-    lanes = shots // SPREAD * channels
+    rows = devices * ROWS * (shots // SPREAD) * channels // LANES
     table = jnp.asarray(dft_tables(radon_size, freq_size))
     return pl.pallas_call(
         functools.partial(dft_kernel, devices),
@@ -84,14 +85,12 @@
             for n in range(step)
         ]
         + [pl.BlockSpec(table.shape, lambda g: (0, 0, 0))],
-        out_specs=pl.BlockSpec((devices * ROWS, 4 * channels), lambda g: (0, g)),
-        out_shape=jax.ShapeDtypeStruct((devices * ROWS, lanes), jnp.float32),
-        scratch_shapes=[pltpu.VMEM((devices * ROWS, LANES), jnp.float32)]
-        * (4 * channels // LANES),
-        compiler_params=pltpu.CompilerParams(vmem_limit_bytes=48 * 2**20),
+        out_specs=pl.BlockSpec(memory_space=pltpu.VMEM),
+        out_shape=jax.ShapeDtypeStruct((rows, LANES), jnp.float32),
+        compiler_params=pltpu.CompilerParams(vmem_limit_bytes=40 * 2**20),
         cost_estimate=pl.CostEstimate(
             flops=3 * table.size * shots * channels,
-            bytes_accessed=4 * (traces.size + devices * ROWS * lanes),
+            bytes_accessed=4 * (traces.size + rows * LANES),
             transcendentals=0,
         ),
     )(*[traces] * step, table)
@@ -125,16 +124,16 @@
     step = pl.program_id(0)
     steps = pl.num_programs(0)
     channels = hi_ref.shape[0] // freq_size
-    slots = rec_refs[0].shape[1] // channels
+    tiles = rec_refs[0].shape[0] // (freq_size * ROWS)
+    slots = tiles * LANES // channels
 
     low = lax.broadcasted_iota(jnp.int32, (ROWS, 2 * channels), 1) < channels
     for r, rec_ref in enumerate(rec_refs):
-        for t in range(slots // 2):
+        for t in range(tiles):
             firsts, seconds = [], []
             for pair in range(freq_size // 2):
-                at = pl.ds(t * 2 * channels, 2 * channels)
-                a = rec_ref[pl.ds(2 * pair * ROWS, ROWS), at]
-                b = rec_ref[pl.ds((2 * pair + 1) * ROWS, ROWS), at]
+                a = rec_ref[pl.ds((2 * pair * tiles + t) * ROWS, ROWS), :]
+                b = rec_ref[pl.ds(((2 * pair + 1) * tiles + t) * ROWS, ROWS), :]
                 firsts.append(jnp.where(low, a, pltpu.roll(b, channels, 1)))
                 seconds.append(jnp.where(low, pltpu.roll(a, channels, 1), b))
             both = jnp.concatenate(
@@ -182,20 +181,17 @@
 
 
 def panel_products(received, weights, lines, sources, panel_rows, freq_size, radon_size):
-    lanes = received.shape[1]
     depth, columns = weights[0].shape
-    channels = depth // freq_size
-    slots = lanes // channels
     grid = 4
     count = radon_size // grid
-    rows = count * slots * ROWS
     shots = sources.shape[1]
+    rows = shots // grid * 2 * BINS
     out = (radon_size, BINS, 2, shots // radon_size, P_SIZE)
     return pl.pallas_call(
         functools.partial(panel_kernel, freq_size, count),
         grid=(grid,),
         in_specs=[
-            pl.BlockSpec((freq_size * ROWS, lanes), lambda r, n=n: (count * r + n, 0))
+            pl.BlockSpec((received.shape[0] // radon_size, LANES), lambda r, n=n: (count * r + n, 0))
             for n in range(count)
         ]
         + [

time: 162 us -> 163 us (level)
  local copies, waits for them, and re-layouts: 6.75 us -> 9.38 us
    all_gather x1, waiting for transfers between devices: 77.6 us -> 71.8 us  [shards(): weights = lax.all_gather(radon_weights, 'freq', axis=0)]
    all_to_all x1, waiting for transfers between devices: 0.01 us -> 5.1 us  [shards(): received = lax.all_to_all(messages, ('radon', 'freq'), 0, 0, tiled=True)]
    unnamed x15 -> x17, local copies, waits for them, and re-layouts: 6.16 us -> 8.78 us
  transfers between devices with their start and end apart: 2 -> 2, of which waited for: 1 -> 2; matrix products, arithmetic and copies ran while one was open for 0% -> 0% of each run, Pallas kernels for 7% -> 7%
where the time goes in v2:
time: 163 us
  waiting for transfers between devices  77.6 us (48%)
  blocking collectives  27 us (17%)
  Pallas kernels  23.6 us (14%)
  between operations  13.5 us (8%)
  starting transfers between devices  11.9 us (7%)
  local copies, waits for them, and re-layouts  9.38 us (6%)
    all_gather x1, waiting for transfers between devices, shards(): weights = lax.all_gather(radon_weights, 'freq', axis=0)  71.8 us
    all_to_all x1, blocking collectives, shards(): result = lax.all_to_all(products, 'radon', 0, 0, tiled=True)  27 us
    all_to_all x1, starting transfers between devices, shards(): received = lax.all_to_all(messages, ('radon', 'freq'), 0, 0, tiled=True)  11.9 us
    pallas_call x1, Pallas kernels, panel_products(): pl.pallas_call(functools.partial(panel_kernel, freq_size, count), grid=(g...  11.9 us
    pallas_call x1, Pallas kernels, dft(): pl.pallas_call(functools.partial(dft_kernel, devices), grid=(shots // ste...  11.5 us
    unnamed x17, local copies, waits for them, and re-layouts  8.78 us
    all_to_all x1, waiting for transfers between devices, shards(): received = lax.all_to_all(messages, ('radon', 'freq'), 0, 0, tiled=True)  5.1 us
  transfers between devices with their start and end apart: 2, of which 2 were waited for; matrix products, arithmetic and copies ran while one was open for 0% of the time, Pallas kernels for 7%

profile of v2, /device:TPU:1, one launch (start us, length us, event | category | flops | bytes accessed | tf_op | source)
XLA Modules:
  0.0 163.1 jit_solution(16004941606369959210)
XLA Ops:
  6.5 0.0 all-gather.3.cloned.1.call-start
  6.5 0.7 all-gather.3.cloned.1.call-update
  7.3 0.0 copy-start.1
  7.3 1.2 copy-done.1
  8.5 11.5 %shard_map.64 = f32[12288,128]{1,0:T(8,128)S(1)} custom-call(f32[48,64,1024]{2,1,0:T(8,128)} %refs_7_.1, f32[48,64,1024]{2,1,0:T(8,128)} %refs_7_.1, f32[48,64,1024]{2,1,0:T(8,128)} %refs_7_.1, f32[48,64,1024]{2,1,0:T(8,128)} %refs_7_.1, f32[48,64,1024]{2,1,0:T(8,128)} %refs_7_.1, f32[48,64,1024]{2,1,0:T(8,128)} %refs_7_.1, f32[48,64,1024]{2,1,0:T(8,128)} %refs_7_.1, ...), custom_call_target="tpu_custom_call" | custom-call | flops 4831838208 | bytes 18874368 | tf_op jit(solution)/shard_map/pallas_call | solution.py:80
  20.0 0.0 copy-start
  20.0 2.6 %copy-done = f32[12288,128]{1,0:T(8,128)} copy-done((f32[12288,128]{1,0:T(8,128)}, f32[12288,128]{1,0:T(8,128)S(1)}, u32[]{:S(2)}) %copy-start) | copy-done | bytes 6291480
  22.6 11.9 %all-to-all-start = ((f32[128,96,128]{2,1,0:T(8,128)}), f32[128,96,128]{2,1,0:T(8,128)}, u32[]{:S(2)}, u32[]{:S(2)}) async-start(f32[128,96,128]{2,1,0:T(8,128)} %bitcast.6), calls=%async_computation | async-start | bytes 12582912 | tf_op jit(solution)/shard_map/all_to_all | solution.py:225
  34.5 0.0 copy-done.7
  34.5 0.1 broadcast_in_dim.30
  34.6 0.2 broadcast_in_dim_reshape.4.refs_4_
  34.9 0.2 copy.11
  35.0 0.1 broadcast_in_dim.35.refs_6_
  35.2 0.1 broadcast_select_fusion
  35.2 71.8 %all-gather.3.cloned.1.call-done = f32[32,64,256]{2,1,0:T(8,128)} async-done(((f32[2,64,256]{2,1,0:T(8,128)}), f32[32,64,256]{2,1,0:T(8,128)}) %all-gather.3.cloned.1.call-update) | async-done | bytes 2097168 | tf_op jit(solution)/shard_map/all_gather | solution.py:222
  107.0 1.6 copy-done.4
  108.6 0.2 shard_map.65
  108.9 0.0 copy-start.2
  108.9 1.0 copy-done.2
  109.8 5.1 %all-to-all-done = f32[128,96,128]{2,1,0:T(8,128)} async-done(((f32[128,96,128]{2,1,0:T(8,128)}), f32[128,96,128]{2,1,0:T(8,128)}, u32[]{:S(2)}, u32[]{:S(2)}) %all-to-all-start) | async-done | bytes 6291488 | tf_op jit(solution)/shard_map/all_to_all | solution.py:225
  114.9 1.2 copy-done.3
  116.2 11.9 %shard_map.66 = f32[8,2,2,48,256]{4,3,2,1,0:T(8,128)S(1)} custom-call(f32[12288,128]{1,0:T(8,128)} %bitcast.1.refs_0_.refs_1_, f32[12288,128]{1,0:T(8,128)} %bitcast.1.refs_0_.refs_1_, bf16[1024,512]{1,0:T(8,128)(2,1)S(1)} %get-tuple-element.7.refs_2_, bf16[1024,512]{1,0:T(8,128)(2,1)S(1)} %copy-done.3, s32[1536,1]{1,0:T(8,128)S(1)} %broadcast_in_dim_reshape.4.refs_4_, ...), custom_call_target="tpu_custom_call" | custom-call | flops 4831838208 | bytes 6291456 | tf_op jit(solution)/shard_map/pallas_call | solution.py:190
  128.1 27.0 %all_to_all.16 = f32[8,2,2,48,256]{4,3,2,1,0:T(8,128)S(1)} all-to-all(f32[8,2,2,48,256]{4,3,2,1,0:T(8,128)S(1)} %shard_map.66), channel_id=1, replica_groups=mesh['radon'=8,'freq'=16] {'radon'}, dimensions={0} | all-to-all | bytes 3145728 | tf_op jit(solution)/shard_map/all_to_all | solution.py:234
  155.1 1.1 copy.15
  (8 shorter events, 0.0 us)
Async XLA Ops:
  6.5 100.5 %all-gather.3.cloned.1.call-start = ((), (), s32[]{:S(2)}) async-start(), calls=%async_computation.2 | async-start | bytes 2228224 | tf_op jit(solution)/shard_map/all_gather | solution.py:222
  7.3 1.2 copy-start.1
  20.0 2.6 %copy-start = (f32[12288,128]{1,0:T(8,128)}, f32[12288,128]{1,0:T(8,128)S(1)}, u32[]{:S(2)}) copy-start(f32[12288,128]{1,0:T(8,128)S(1)} %shard_map.64) | copy-start | bytes 18874372
  22.6 11.9 %copy-start.7 = (s32[384]{0:T(512)S(1)}, s32[384]{0:T(512)}, u32[]{:S(2)}) copy-start(s32[384]{0:T(512)} %param.9) | copy-start | bytes 4612
  22.6 12.3 %copy-start.5 = (f32[384,256]{1,0:T(8,128)S(1)}, f32[384,256]{1,0:T(8,128)}, u32[]{:S(2)}) copy-start(f32[384,256]{1,0:T(8,128)} %param.8) | copy-start | bytes 1179652
  22.6 12.4 %copy-start.6 = (s32[384]{0:T(512)S(1)}, s32[384]{0:T(512)}, u32[]{:S(2)}) copy-start(s32[384]{0:T(512)} %param.10) | copy-start | bytes 4612
  22.6 92.3 %all-to-all-start = ((f32[128,96,128]{2,1,0:T(8,128)}), f32[128,96,128]{2,1,0:T(8,128)}, u32[]{:S(2)}, u32[]{:S(2)}) async-start(f32[128,96,128]{2,1,0:T(8,128)} %bitcast.6), calls=%async_computation | async-start | bytes 12582912 | tf_op jit(solution)/shard_map/all_to_all | solution.py:225
  107.0 1.6 copy-start.4
  108.9 1.0 copy-start.2
  114.9 1.2 copy-start.3
Sparse Core Ops, SparseCore 0:
  9.8 97.1 all-gather.2

commit v3 on v2

v3 whole, which is shorter than its diff:
```python
import functools

import jax
import jax.numpy as jnp
import ml_dtypes
import numpy as np
from jax import lax
from jax.experimental import pallas as pl
from jax.experimental.pallas import tpu as pltpu
from jax.sharding import PartitionSpec as P

NT = 1024
NF = 256
P_SIZE = 256
L = 2
K = 2
HALF = NT // 2
LANES = 128
BINS = 2
ROWS = 8
SPREAD = ROWS // 2


def split(x):
    hi = x.astype(jnp.bfloat16)
    lo = (x - hi.astype(jnp.float32)).astype(jnp.bfloat16)
    return hi, lo


def dot3(a, b):
    dot = functools.partial(jnp.dot, preferred_element_type=jnp.float32)
    return dot(a[0], b[0]) + (dot(a[0], b[1]) + dot(a[1], b[0]))


def dft_tables(radon_size, freq_size):
    band = NF // freq_size
    device = np.arange(radon_size * freq_size)
    rows = []
    for parity in range(BINS):
        bins = band * (device % freq_size) + BINS * (device // freq_size) + parity
        phase = (bins[:, None] * np.arange(HALF)[None, :] % NT) * (2.0 * np.pi / NT)
        rows += [np.cos(phase), -np.sin(phase)]
    table = (np.concatenate(rows) * NT ** (-0.5)).astype(np.float32)
    hi = table.astype(ml_dtypes.bfloat16)
    lo = (table - hi.astype(np.float32)).astype(ml_dtypes.bfloat16)
    return np.concatenate([hi, lo, hi], axis=1)


def dft_kernel(*refs):
    x_refs, (table_ref, out_ref), folded = refs[:2], refs[2:4], refs[4:]
    devices = out_ref.shape[0]
    groups, channels, _ = x_refs[0].shape
    message = BINS * ROWS
    flat_ref = out_ref.reshape(devices * message, LANES)
    for half in range(2):
        for parity in range(BINS):
            rows_ref = folded[half * BINS + parity]
            for n in range(2):
                for i in range(2):
                    shot = x_refs[i][half * 2 + n]
                    head, tail = shot[:, :HALF], shot[:, HALF:]
                    hi, lo = split(head - tail if parity else head + tail)
                    at = pl.ds((n * 2 + i) * channels, channels)
                    rows_ref[at, :HALF] = hi
                    rows_ref[at, HALF : 2 * HALF] = hi
                    rows_ref[at, 2 * HALF :] = lo
            at = slice(2 * parity * devices, 2 * (parity + 1) * devices)
            spectrum = lax.dot_general(
                table_ref[at],
                rows_ref[...],
                (((1,), (1,)), ((), ())),
                preferred_element_type=jnp.float32,
            )
            for n in range(2):
                for part in range(2):
                    row = parity * ROWS + 2 * (half * 2 + n) + part
                    flat_ref[pl.ds(row, devices, stride=message), :] = spectrum[
                        part * devices : (part + 1) * devices, n * LANES : (n + 1) * LANES
                    ]


def dft(traces, radon_size, freq_size):
    shots, channels, _ = traces.shape
    devices = radon_size * freq_size
    step = LANES // channels * SPREAD
    out = (devices, BINS, shots // step * ROWS, LANES)
    table = jnp.asarray(dft_tables(radon_size, freq_size))
    return pl.pallas_call(
        dft_kernel,
        grid=(shots // step,),
        in_specs=[
            pl.BlockSpec((step // 2, channels, NT), lambda g, n=n: (2 * g + n, 0, 0))
            for n in range(2)
        ]
        + [pl.BlockSpec(table.shape, lambda g: (0, 0))],
        out_specs=pl.BlockSpec((devices, BINS, ROWS, LANES), lambda g: (0, 0, g, 0)),
        out_shape=jax.ShapeDtypeStruct(out, jnp.float32),
        scratch_shapes=[pltpu.VMEM((4 * channels, 3 * HALF), jnp.bfloat16)] * (2 * BINS),
        compiler_params=pltpu.CompilerParams(vmem_limit_bytes=48 * 2**20),
        cost_estimate=pl.CostEstimate(
            flops=2 * table.size * shots * channels,
            bytes_accessed=6 * traces.size,
            transcendentals=0,
        ),
    )(traces, traces, table)


def weights_kernel(w_ref, out_ref):
    channels = w_ref.shape[2]
    for j in range(w_ref.shape[0]):
        for line in range(L):
            at = (pl.ds(j * channels, channels), pl.ds(line * P_SIZE, P_SIZE))
            hi, lo = split(w_ref[j, line])
            out_ref[0, at[0], at[1]] = hi
            out_ref[1, at[0], at[1]] = lo


def split_weights(weights):
    freq_size, _, channels, _ = weights.shape
    return pl.pallas_call(
        weights_kernel,
        out_shape=jax.ShapeDtypeStruct(
            (2, freq_size * channels, L * P_SIZE), jnp.bfloat16
        ),
        compiler_params=pltpu.CompilerParams(vmem_limit_bytes=32 * 2**20),
        cost_estimate=pl.CostEstimate(
            flops=10**11, bytes_accessed=8 * weights.size, transcendentals=0
        ),
    )(weights)


def panel_kernel(count, *refs):
    rec_refs, refs = refs[:count], refs[count:]
    (w_ref, line_ref, src_ref, panel_ref, out_ref, a_hi, a_lo), gathers = refs[:7], refs[7:]
    step = pl.program_id(0)
    steps = pl.num_programs(0)
    freq_size, bins, height, _ = rec_refs[0].shape
    channels = w_ref.shape[1] // freq_size
    tiles = height // ROWS

    low = lax.broadcasted_iota(jnp.int32, (ROWS, LANES), 1) < channels
    for parity in range(bins):
        for r, rec_ref in enumerate(rec_refs):
            for t in range(tiles):
                firsts, seconds = [], []
                for j in range(0, freq_size, 2):
                    a = rec_ref[j, parity, pl.ds(t * ROWS, ROWS), :]
                    b = rec_ref[j + 1, parity, pl.ds(t * ROWS, ROWS), :]
                    firsts.append(jnp.where(low, a, pltpu.roll(b, channels, 1)))
                    seconds.append(jnp.where(low, pltpu.roll(a, channels, 1), b))
                both = jnp.concatenate(
                    [jnp.concatenate(firsts, axis=1), jnp.concatenate(seconds, axis=1)], axis=0
                )
                at = pl.ds(((parity * count + r) * tiles + t) * 2 * ROWS, 2 * ROWS)
                a_hi[at, :], a_lo[at, :] = split(both)
    lines = dot3((a_hi[...], a_lo[...]), (w_ref[0], w_ref[1]))
    rows = a_hi.shape[0] // bins
    first_line = line_ref[...] == 0
    for parity in range(bins):
        own = lines[parity * rows : (parity + 1) * rows]
        chosen = jnp.where(first_line, own[:, :P_SIZE], own[:, P_SIZE:])
        for h in range(P_SIZE // LANES):
            gathers[parity * (P_SIZE // LANES) + h][
                pl.ds(pl.multiple_of(step * rows, rows), rows), :
            ] = chosen[:, h * LANES : (h + 1) * LANES]

    @pl.when(step == steps - 1)
    def _():
        shots = src_ref.shape[1]
        own = shots // out_ref.shape[0]
        source = split(src_ref[...])
        first = panel_ref[...] == 0
        for parity in range(bins):
            left, panels = ([], []), []
            for part in range(2):
                at = pl.ds(part, shots, stride=2)
                both = jnp.concatenate(
                    [
                        gathers[parity * (P_SIZE // LANES) + h][at, :]
                        for h in range(P_SIZE // LANES)
                    ],
                    axis=1,
                )
                panels.append(split(dot3(source, split(both))))
                for k in range(K):
                    hi, lo = split(jnp.where(first == (k == 0), both, 0.0))
                    left[0].append(hi)
                    left[1].append(lo)
            left = [jnp.concatenate(pieces, axis=1) for pieces in left]
            real, imag = panels
            rights = (
                [jnp.concatenate([real[n], -imag[n]], axis=0) for n in range(2)],
                [jnp.concatenate([imag[n], real[n]], axis=0) for n in range(2)],
            )
            for part in range(2):
                product = dot3(left, rights[part])
                for r in range(out_ref.shape[0]):
                    out_ref[r, parity, part] = product[r * own : (r + 1) * own]


def panel_products(received, weights, lines, sources, panel_rows, radon_size):
    _, depth, columns = weights.shape
    freq_size = received.shape[0] // radon_size
    grid = 4
    count = radon_size // grid
    shots = sources.shape[1]
    rows = shots // grid * 2
    out = (radon_size, BINS, 2, shots // radon_size, P_SIZE)
    return pl.pallas_call(
        functools.partial(panel_kernel, count),
        grid=(grid,),
        in_specs=[
            pl.BlockSpec(
                (freq_size,) + received.shape[1:], lambda r, n=n: (count * r + n, 0, 0, 0)
            )
            for n in range(count)
        ]
        + [
            pl.BlockSpec(weights.shape, lambda r: (0, 0, 0)),
            pl.BlockSpec((rows, 1), lambda r: (r, 0)),
            pl.BlockSpec(sources.shape, lambda r: (0, 0)),
            pl.BlockSpec((shots, 1), lambda r: (0, 0)),
        ],
        out_specs=pl.BlockSpec(out, lambda r: (0, 0, 0, 0, 0)),
        out_shape=jax.ShapeDtypeStruct(out, jnp.float32),
        scratch_shapes=[pltpu.VMEM((BINS * rows, depth), jnp.bfloat16)] * 2
        + [pltpu.VMEM((grid * rows, LANES), jnp.float32)] * (BINS * P_SIZE // LANES),
        compiler_params=pltpu.CompilerParams(vmem_limit_bytes=48 * 2**20),
        cost_estimate=pl.CostEstimate(
            flops=6 * grid * BINS * rows * depth * columns,
            bytes_accessed=4 * received.size,
            transcendentals=0,
        ),
    )(*[received] * count, weights, lines, sources, panel_rows)


def shards(shot_traces, radon_weights, source_weights, line_index, panel_index):
    shot_rows = shot_traces.shape[0]
    freq_size = lax.axis_size("freq")
    radon_size = lax.axis_size("radon")

    weights = split_weights(lax.all_gather(radon_weights, "freq", axis=0))
    messages = dft(shot_traces, radon_size, freq_size)
    received = lax.all_to_all(messages, ("radon", "freq"), 0, 0, tiled=True)

    lines = jnp.repeat(line_index, 2)[:, None]
    onehot = panel_index[None, :] == jnp.arange(K, dtype=jnp.int32)[:, None]
    sources = jnp.where(onehot[:, None, :], source_weights.T[None], 0.0).reshape(K * P_SIZE, -1)

    products = panel_products(
        received, weights, lines, sources, panel_index[:, None], radon_size
    )
    result = lax.all_to_all(products, "radon", 0, 0, tiled=True)
    return result.reshape(radon_size * BINS, 2, shot_rows, P_SIZE)


def solution(mesh):
    placed = (P("radon", "freq", None), P(None, "freq", None), P(), P(), P())
    return jax.shard_map(
        shards,
        mesh=mesh,
        in_specs=placed,
        out_specs=P("freq", None, "radon", None),
        check_vma=False,
    )
```

time: 163 us -> 159 us (0.975)
  local copies, waits for them, and re-layouts: 9.38 us -> 4.65 us
  waiting for transfers between devices: 77.6 us -> 80.6 us
  blocking collectives: 27 us -> 24.7 us
    all_gather x1, waiting for transfers between devices: 71.8 us -> 77.7 us  [shards(): weights = split_weights(lax.all_gather(radon_weights, 'freq', axis=0))]
    unnamed x17 -> x11, local copies, waits for them, and re-layouts: 8.78 us -> 4.15 us
    all_to_all x1, waiting for transfers between devices: 5.1 us -> 2.18 us  [shards(): received = lax.all_to_all(messages, ('radon', 'freq'), 0, 0, tiled=True)]
    all_to_all x1, blocking collectives: 27 us -> 24.7 us  [shards(): result = lax.all_to_all(products, 'radon', 0, 0, tiled=True)]
where the time goes in v3:
time: 159 us
  waiting for transfers between devices  80.6 us (51%)
  blocking collectives  24.7 us (16%)
  Pallas kernels  23.5 us (15%)
  between operations  13.5 us (8%)
  starting transfers between devices  11.9 us (7%)
  local copies, waits for them, and re-layouts  4.65 us (3%)
    all_gather x1, waiting for transfers between devices, shards(): weights = split_weights(lax.all_gather(radon_weights, 'freq', axis=0))  77.7 us
    all_to_all x1, blocking collectives, shards(): result = lax.all_to_all(products, 'radon', 0, 0, tiled=True)  24.7 us
    all_to_all x1, starting transfers between devices, shards(): received = lax.all_to_all(messages, ('radon', 'freq'), 0, 0, tiled=True)  11.9 us
    pallas_call x1, Pallas kernels, dft(): pl.pallas_call(dft_kernel, grid=(shots // step,), in_specs=[pl.BlockSpec(...  11.6 us
    pallas_call x1, Pallas kernels, panel_products(): pl.pallas_call(functools.partial(panel_kernel, count), grid=(grid,), in_s...  11.6 us
    unnamed x11, local copies, waits for them, and re-layouts  4.15 us
  transfers between devices with their start and end apart: 2, of which 2 were waited for; matrix products, arithmetic and copies ran while one was open for 0% of the time, Pallas kernels for 7%

profile of v3, /device:TPU:1, one launch (start us, length us, event | category | flops | bytes accessed | tf_op | source)
XLA Modules:
  0.0 158.9 jit_solution(16641495477189329630)
XLA Ops:
  6.5 0.0 all-gather.3.cloned.1.call-start
  6.5 0.7 all-gather.3.cloned.1.call-update
  7.3 0.0 copy-start
  7.3 1.4 copy-done
  8.7 11.6 %shard_map.64 = f32[128,2,48,128]{3,2,1,0:T(8,128)} custom-call(f32[48,64,1024]{2,1,0:T(8,128)} %refs_1_.1, f32[48,64,1024]{2,1,0:T(8,128)} %refs_1_.1, bf16[512,1536]{1,0:T(8,128)(2,1)S(1)} %copy-done), custom_call_target="tpu_custom_call" | custom-call | flops 4831838208 | bytes 18874368 | tf_op jit(solution)/shard_map/pallas_call | solution.py:88
  20.3 0.0 copy-start.2
  20.3 0.0 copy-start.3
  20.3 11.9 %all-to-all-start = ((f32[128,2,48,128]{3,2,1,0:T(8,128)}), f32[128,2,48,128]{3,2,1,0:T(8,128)}, u32[]{:S(2)}, u32[]{:S(2)}) async-start(f32[128,2,48,128]{3,2,1,0:T(8,128)} %shard_map.64), calls=%async_computation | async-start | bytes 12582912 | tf_op jit(solution)/shard_map/all_to_all | solution.py:244
  32.2 0.0 copy-done.2
  32.2 0.2 copy.11
  32.4 0.0 copy-done.4
  32.4 0.1 broadcast_in_dim.30
  32.5 0.1 broadcast_in_dim_reshape.4.refs_3_
  32.7 0.0 copy-done.3
  32.7 0.1 broadcast_in_dim.35.refs_5_
  32.8 0.1 broadcast_select_fusion
  32.9 77.7 %all-gather.3.cloned.1.call-done = f32[32,64,256]{2,1,0:T(8,128)} async-done(((f32[2,64,256]{2,1,0:T(8,128)}), f32[32,64,256]{2,1,0:T(8,128)}) %all-gather.3.cloned.1.call-update) | async-done | bytes 2097168 | tf_op jit(solution)/shard_map/all_gather | solution.py:242
  110.6 0.0 copy-start.1
  110.6 1.6 copy-done.1
  112.2 0.2 shard_map.65.refs_2_
  112.4 2.2 %all-to-all-done.refs_0_.refs_1_ = f32[128,2,48,128]{3,2,1,0:T(8,128)} async-done(((f32[128,2,48,128]{3,2,1,0:T(8,128)}), f32[128,2,48,128]{3,2,1,0:T(8,128)}, u32[]{:S(2)}, u32[]{:S(2)}) %all-to-all-start) | async-done | bytes 6291488 | tf_op jit(solution)/shard_map/all_to_all | solution.py:244
  114.6 11.6 %shard_map.66 = f32[8,2,2,48,256]{4,3,2,1,0:T(8,128)S(1)} custom-call(f32[128,2,48,128]{3,2,1,0:T(8,128)} %all-to-all-done.refs_0_.refs_1_, f32[128,2,48,128]{3,2,1,0:T(8,128)} %all-to-all-done.refs_0_.refs_1_, bf16[2,1024,512]{2,1,0:T(8,128)(2,1)S(1)} %shard_map.65.refs_2_, s32[768,1]{1,0:T(8,128)S(1)} %broadcast_in_dim_reshape.4.refs_3_, ...), custom_call_target="tpu_custom_call" | custom-call | flops 4831838208 | bytes 6291456 | tf_op jit(solution)/shard_map/pallas_call | solution.py:209
  126.2 24.7 %all_to_all.10 = f32[8,2,2,48,256]{4,3,2,1,0:T(8,128)S(1)} all-to-all(f32[8,2,2,48,256]{4,3,2,1,0:T(8,128)S(1)} %shard_map.66), channel_id=1, replica_groups=mesh['radon'=8,'freq'=16] {'radon'}, dimensions={0} | all-to-all | bytes 3145728 | tf_op jit(solution)/shard_map/all_to_all | solution.py:253
  150.9 1.1 copy.15
  (2 shorter events, 0.0 us)
Async XLA Ops:
  6.5 104.0 %all-gather.3.cloned.1.call-start = ((), (), s32[]{:S(2)}) async-start(), calls=%async_computation.2 | async-start | bytes 2228224 | tf_op jit(solution)/shard_map/all_gather | solution.py:242
  7.3 1.4 copy-start
  20.3 11.9 %copy-start.2 = (f32[384,256]{1,0:T(8,128)S(1)}, f32[384,256]{1,0:T(8,128)}, u32[]{:S(2)}) copy-start(f32[384,256]{1,0:T(8,128)} %param.8) | copy-start | bytes 1179652
  20.3 12.1 %copy-start.4 = (s32[384]{0:T(512)S(1)}, s32[384]{0:T(512)}, u32[]{:S(2)}) copy-start(s32[384]{0:T(512)} %param.9) | copy-start | bytes 4612
  20.3 12.4 %copy-start.3 = (s32[384]{0:T(512)S(1)}, s32[384]{0:T(512)}, u32[]{:S(2)}) copy-start(s32[384]{0:T(512)} %param.10) | copy-start | bytes 4612
  20.3 94.3 %all-to-all-start = ((f32[128,2,48,128]{3,2,1,0:T(8,128)}), f32[128,2,48,128]{3,2,1,0:T(8,128)}, u32[]{:S(2)}, u32[]{:S(2)}) async-start(f32[128,2,48,128]{3,2,1,0:T(8,128)} %shard_map.64), calls=%async_computation | async-start | bytes 12582912 | tf_op jit(solution)/shard_map/all_to_all | solution.py:244
  110.6 1.6 %copy-start.1 = (f32[32,64,256]{2,1,0:T(8,128)S(1)}, f32[32,64,256]{2,1,0:T(8,128)}, u32[]{:S(2)}) copy-start(f32[32,64,256]{2,1,0:T(8,128)} %all-gather.3.cloned.1.call-done) | copy-start | bytes 6291460
Sparse Core Ops, SparseCore 0:
  9.8 100.7 all-gather.2

commit v4 on v3

--- a/solution.py
+++ b/solution.py
@@ -46,63 +46,96 @@
     return np.concatenate([hi, lo, hi], axis=1)
 
 
-def dft_kernel(*refs):
-    x_refs, (table_ref, out_ref), folded = refs[:2], refs[2:4], refs[4:]
-    devices = out_ref.shape[0]
-    groups, channels, _ = x_refs[0].shape
+def dft_kernel(x_hbm, table_hbm, out_hbm, x_buf, table, out_buf, *refs):
+    folded, (x_sems, table_sem, out_sems) = refs[:-3], refs[-3:]
+    steps, devices = out_buf.shape[:2]
+    pieces, shots, channels, _ = x_buf.shape
     message = BINS * ROWS
-    flat_ref = out_ref.reshape(devices * message, LANES)
-    for half in range(2):
-        for parity in range(BINS):
-            rows_ref = folded[half * BINS + parity]
-            for n in range(2):
-                for i in range(2):
-                    shot = x_refs[i][half * 2 + n]
-                    head, tail = shot[:, :HALF], shot[:, HALF:]
-                    hi, lo = split(head - tail if parity else head + tail)
-                    at = pl.ds((n * 2 + i) * channels, channels)
-                    rows_ref[at, :HALF] = hi
-                    rows_ref[at, HALF : 2 * HALF] = hi
-                    rows_ref[at, 2 * HALF :] = lo
-            at = slice(2 * parity * devices, 2 * (parity + 1) * devices)
-            spectrum = lax.dot_general(
-                table_ref[at],
-                rows_ref[...],
-                (((1,), (1,)), ((), ())),
-                preferred_element_type=jnp.float32,
-            )
-            for n in range(2):
-                for part in range(2):
-                    row = parity * ROWS + 2 * (half * 2 + n) + part
-                    flat_ref[pl.ds(row, devices, stride=message), :] = spectrum[
-                        part * devices : (part + 1) * devices, n * LANES : (n + 1) * LANES
-                    ]
+
+    table_copy = pltpu.make_async_copy(table_hbm, table, table_sem)
+    table_copy.start()
+
+    def x_copy(n):
+        return pltpu.make_async_copy(
+            x_hbm.at[pl.ds(n * shots, shots)], x_buf.at[n], x_sems.at[n]
+        )
+
+    for n in range(pieces):
+        x_copy(n).start()
+    table_copy.wait()
+
+    def out_copy(g):
+        return pltpu.make_async_copy(
+            out_buf.at[g], out_hbm.at[:, :, pl.ds(g * ROWS, ROWS), :], out_sems.at[g]
+        )
+
+    def body(g, carry):
+        x_copy(2 * g).wait()
+        x_copy(2 * g + 1).wait()
+        flat_ref = out_buf.at[g].reshape(devices * message, LANES)
+        for half in range(2):
+            for parity in range(BINS):
+                rows_ref = folded[half * BINS + parity]
+                for n in range(2):
+                    for i in range(2):
+                        shot = x_buf[2 * g + i, half * 2 + n]
+                        head, tail = shot[:, :HALF], shot[:, HALF:]
+                        hi, lo = split(head - tail if parity else head + tail)
+                        at = pl.ds((n * 2 + i) * channels, channels)
+                        rows_ref[at, :HALF] = hi
+                        rows_ref[at, HALF : 2 * HALF] = hi
+                        rows_ref[at, 2 * HALF :] = lo
+                at = slice(2 * parity * devices, 2 * (parity + 1) * devices)
+                spectrum = lax.dot_general(
+                    table[at],
+                    rows_ref[...],
+                    (((1,), (1,)), ((), ())),
+                    preferred_element_type=jnp.float32,
+                )
+                for n in range(2):
+                    for part in range(2):
+                        row = parity * ROWS + 2 * (half * 2 + n) + part
+                        flat_ref[pl.ds(row, devices, stride=message), :] = spectrum[
+                            part * devices : (part + 1) * devices, n * LANES : (n + 1) * LANES
+                        ]
+        out_copy(g).start()
+        return carry
+
+    lax.fori_loop(0, steps, body, 0)
+    for g in range(steps):
+        out_copy(g).wait()
 
 
 def dft(traces, radon_size, freq_size):
     shots, channels, _ = traces.shape
     devices = radon_size * freq_size
     step = LANES // channels * SPREAD
-    out = (devices, BINS, shots // step * ROWS, LANES)
+    steps = shots // step
     table = jnp.asarray(dft_tables(radon_size, freq_size))
+    any_space = pl.BlockSpec(memory_space=pl.ANY)
     return pl.pallas_call(
         dft_kernel,
-        grid=(shots // step,),
-        in_specs=[
-            pl.BlockSpec((step // 2, channels, NT), lambda g, n=n: (2 * g + n, 0, 0))
-            for n in range(2)
+        in_specs=[any_space, any_space],
+        out_specs=any_space,
+        out_shape=jax.ShapeDtypeStruct((devices, BINS, steps * ROWS, LANES), jnp.float32),
+        scratch_shapes=[
+            pltpu.VMEM((2 * steps, step // 2, channels, NT), jnp.float32),
+            pltpu.VMEM(table.shape, table.dtype),
+            pltpu.VMEM((steps, devices, BINS, ROWS, LANES), jnp.float32),
         ]
-        + [pl.BlockSpec(table.shape, lambda g: (0, 0))],
-        out_specs=pl.BlockSpec((devices, BINS, ROWS, LANES), lambda g: (0, 0, g, 0)),
-        out_shape=jax.ShapeDtypeStruct(out, jnp.float32),
-        scratch_shapes=[pltpu.VMEM((4 * channels, 3 * HALF), jnp.bfloat16)] * (2 * BINS),
-        compiler_params=pltpu.CompilerParams(vmem_limit_bytes=48 * 2**20),
+        + [pltpu.VMEM((4 * channels, 3 * HALF), jnp.bfloat16)] * (2 * BINS)
+        + [
+            pltpu.SemaphoreType.DMA((2 * steps,)),
+            pltpu.SemaphoreType.DMA,
+            pltpu.SemaphoreType.DMA((steps,)),
+        ],
+        compiler_params=pltpu.CompilerParams(vmem_limit_bytes=60 * 2**20),
         cost_estimate=pl.CostEstimate(
             flops=2 * table.size * shots * channels,
             bytes_accessed=6 * traces.size,
             transcendentals=0,
         ),
-    )(traces, traces, table)
+    )(traces, table)
 
 
 def weights_kernel(w_ref, out_ref):
@@ -201,7 +234,7 @@
 def panel_products(received, weights, lines, sources, panel_rows, radon_size):
     _, depth, columns = weights.shape
     freq_size = received.shape[0] // radon_size
-    grid = 4
+    grid = 2
     count = radon_size // grid
     shots = sources.shape[1]
     rows = shots // grid * 2

time: 159 us -> 159 us (level)
  Pallas kernels: 23.5 us -> 25.3 us
    pallas_call x1, Pallas kernels: 11.6 us -> 13.4 us  [dft(): pl.pallas_call(dft_kernel, in_specs=[any_space, any_space], out_specs=any...]
    unnamed x11 -> x9, local copies, waits for them, and re-layouts: 4.15 us -> 2.75 us
  transfers between devices with their start and end apart: 2 -> 2, of which waited for: 2 -> 2; matrix products, arithmetic and copies ran while one was open for 0% -> 0% of each run, Pallas kernels for 7% -> 9%
where the time goes in v4:
time: 159 us
  waiting for transfers between devices  80.8 us (51%)
  Pallas kernels  25.3 us (16%)
  blocking collectives  24.3 us (15%)
  between operations  13.5 us (8%)
  starting transfers between devices  11.9 us (7%)
  local copies, waits for them, and re-layouts  3.25 us (2%)
    all_gather x1, waiting for transfers between devices, shards(): weights = split_weights(lax.all_gather(radon_weights, 'freq', axis=0))  76.3 us
    all_to_all x1, blocking collectives, shards(): result = lax.all_to_all(products, 'radon', 0, 0, tiled=True)  24.3 us
    pallas_call x1, Pallas kernels, dft(): pl.pallas_call(dft_kernel, in_specs=[any_space, any_space], out_specs=any...  13.4 us
    all_to_all x1, starting transfers between devices, shards(): received = lax.all_to_all(messages, ('radon', 'freq'), 0, 0, tiled=True)  11.9 us
    pallas_call x1, Pallas kernels, panel_products(): pl.pallas_call(functools.partial(panel_kernel, count), grid=(grid,), in_s...  11.6 us
    all_to_all x1, waiting for transfers between devices, shards(): received = lax.all_to_all(messages, ('radon', 'freq'), 0, 0, tiled=True)  3.73 us
  transfers between devices with their start and end apart: 2, of which 2 were waited for; matrix products, arithmetic and copies ran while one was open for 0% of the time, Pallas kernels for 9%

profile of v4, /device:TPU:1, one launch (start us, length us, event | category | flops | bytes accessed | tf_op | source)
XLA Modules:
  0.0 159.1 jit_solution(10757531912784568118)
XLA Ops:
  6.5 0.0 all-gather.3.cloned.1.call-start
  6.5 0.7 all-gather.3.cloned.1.call-update
  7.3 13.4 %shard_map.64 = f32[128,2,48,128]{3,2,1,0:T(8,128)} custom-call(f32[48,64,1024]{2,1,0:T(8,128)} %x_hbm.1, bf16[512,1536]{1,0:T(8,128)(2,1)} %constant.4.clone.table_hbm), custom_call_target="tpu_custom_call" | custom-call | flops 4831838208 | bytes 18874368 | tf_op jit(solution)/shard_map/pallas_call | solution.py:116
  20.7 0.0 copy-start.1
  20.7 0.0 copy-start.3
  20.7 0.0 copy-start.2
  20.7 11.9 %all-to-all-start = ((f32[128,2,48,128]{3,2,1,0:T(8,128)}), f32[128,2,48,128]{3,2,1,0:T(8,128)}, u32[]{:S(2)}, u32[]{:S(2)}) async-start(f32[128,2,48,128]{3,2,1,0:T(8,128)} %shard_map.64), calls=%async_computation | async-start | bytes 12582912 | tf_op jit(solution)/shard_map/all_to_all | solution.py:277
  32.6 0.0 copy-done.1
  32.7 0.2 copy.11
  32.8 0.0 copy-done.3
  32.8 0.1 broadcast_in_dim.30
  33.0 0.1 broadcast_in_dim_reshape.4.refs_5_
  33.1 0.0 copy-done.2
  33.1 0.1 broadcast_in_dim.35.refs_7_
  33.2 0.1 broadcast_select_fusion
  33.3 76.3 %all-gather.3.cloned.1.call-done = f32[32,64,256]{2,1,0:T(8,128)} async-done(((f32[2,64,256]{2,1,0:T(8,128)}), f32[32,64,256]{2,1,0:T(8,128)}) %all-gather.3.cloned.1.call-update) | async-done | bytes 2097168 | tf_op jit(solution)/shard_map/all_gather | solution.py:275
  109.6 0.0 copy-start
  109.6 1.6 copy-done
  111.2 0.2 shard_map.65.refs_4_
  111.5 3.7 %all-to-all-done.refs_0_.refs_1_.refs_2_.refs_3_ = f32[128,2,48,128]{3,2,1,0:T(8,128)} async-done(((f32[128,2,48,128]{3,2,1,0:T(8,128)}), f32[128,2,48,128]{3,2,1,0:T(8,128)}, u32[]{:S(2)}, u32[]{:S(2)}) %all-to-all-start) | async-done | bytes 6291488 | tf_op jit(solution)/shard_map/all_to_all | solution.py:277
  115.2 11.6 %shard_map.66 = f32[8,2,2,48,256]{4,3,2,1,0:T(8,128)S(1)} custom-call(f32[128,2,48,128]{3,2,1,0:T(8,128)} %all-to-all-done.refs_0_.refs_1_.refs_2_.refs_3_, f32[128,2,48,128]{3,2,1,0:T(8,128)} %all-to-all-done.refs_0_.refs_1_.refs_2_.refs_3_, f32[128,2,48,128]{3,2,1,0:T(8,128)} %all-to-all-done.refs_0_.refs_1_.refs_2_.refs_3_, ...), custom_call_target="tpu_custom_call" | custom-call | flops 4831838208 | bytes 6291456 | tf_op jit(solution)/shard_map/pallas_call | solution.py:242
  126.8 24.3 %all_to_all.10 = f32[8,2,2,48,256]{4,3,2,1,0:T(8,128)S(1)} all-to-all(f32[8,2,2,48,256]{4,3,2,1,0:T(8,128)S(1)} %shard_map.66), channel_id=1, replica_groups=mesh['radon'=8,'freq'=16] {'radon'}, dimensions={0} | all-to-all | bytes 3145728 | tf_op jit(solution)/shard_map/all_to_all | solution.py:286
  151.1 1.1 copy.15
  (1 shorter events, 0.0 us)
Async XLA Ops:
  6.5 103.1 %all-gather.3.cloned.1.call-start = ((), (), s32[]{:S(2)}) async-start(), calls=%async_computation.2 | async-start | bytes 2228224 | tf_op jit(solution)/shard_map/all_gather | solution.py:275
  20.7 12.0 %copy-start.1 = (f32[384,256]{1,0:T(8,128)S(1)}, f32[384,256]{1,0:T(8,128)}, u32[]{:S(2)}) copy-start(f32[384,256]{1,0:T(8,128)} %param.8) | copy-start | bytes 1179652
  20.7 12.1 %copy-start.3 = (s32[384]{0:T(512)S(1)}, s32[384]{0:T(512)}, u32[]{:S(2)}) copy-start(s32[384]{0:T(512)} %param.9) | copy-start | bytes 4612
  20.7 12.4 %copy-start.2 = (s32[384]{0:T(512)S(1)}, s32[384]{0:T(512)}, u32[]{:S(2)}) copy-start(s32[384]{0:T(512)} %param.10) | copy-start | bytes 4612
  20.7 94.5 %all-to-all-start = ((f32[128,2,48,128]{3,2,1,0:T(8,128)}), f32[128,2,48,128]{3,2,1,0:T(8,128)}, u32[]{:S(2)}, u32[]{:S(2)}) async-start(f32[128,2,48,128]{3,2,1,0:T(8,128)} %shard_map.64), calls=%async_computation | async-start | bytes 12582912 | tf_op jit(solution)/shard_map/all_to_all | solution.py:277
  109.6 1.6 %copy-start = (f32[32,64,256]{2,1,0:T(8,128)S(1)}, f32[32,64,256]{2,1,0:T(8,128)}, u32[]{:S(2)}) copy-start(f32[32,64,256]{2,1,0:T(8,128)} %all-gather.3.cloned.1.call-done) | copy-start | bytes 6291460
Sparse Core Ops, SparseCore 0:
  9.8 99.7 all-gather.2

commit v5 on v4

--- a/solution.py
+++ b/solution.py
@@ -39,18 +39,28 @@
     for parity in range(BINS):
         bins = band * (device % freq_size) + BINS * (device // freq_size) + parity
         phase = (bins[:, None] * np.arange(HALF)[None, :] % NT) * (2.0 * np.pi / NT)
-        rows += [np.cos(phase), -np.sin(phase)]
+        rows.append(np.stack([np.cos(phase), -np.sin(phase)], axis=1).reshape(-1, HALF))
     table = (np.concatenate(rows) * NT ** (-0.5)).astype(np.float32)
     hi = table.astype(ml_dtypes.bfloat16)
     lo = (table - hi.astype(np.float32)).astype(ml_dtypes.bfloat16)
     return np.concatenate([hi, lo, hi], axis=1)
 
 
+def trade(pieces, block):
+    first, second = pieces
+    row = lax.broadcasted_iota(jnp.int32, first.shape, 1)
+    stay = lax.rem(lax.div(row, block), 2) == 0
+    return (
+        jnp.where(stay, first, pltpu.roll(second, block, 1)),
+        jnp.where(stay, pltpu.roll(first, ROWS - block, 1), second),
+    )
+
+
 def dft_kernel(x_hbm, table_hbm, out_hbm, x_buf, table, out_buf, *refs):
     folded, (x_sems, table_sem, out_sems) = refs[:-3], refs[-3:]
-    steps, devices = out_buf.shape[:2]
+    steps = out_buf.shape[0]
     pieces, shots, channels, _ = x_buf.shape
-    message = BINS * ROWS
+    count = table.shape[0] // BINS
 
     table_copy = pltpu.make_async_copy(table_hbm, table, table_sem)
     table_copy.start()
@@ -66,38 +76,40 @@
 
     def out_copy(g):
         return pltpu.make_async_copy(
-            out_buf.at[g], out_hbm.at[:, :, pl.ds(g * ROWS, ROWS), :], out_sems.at[g]
+            out_buf.at[g], out_hbm.at[:, :, :, pl.ds(g * ROWS, ROWS), :], out_sems.at[g]
         )
 
     def body(g, carry):
         x_copy(2 * g).wait()
         x_copy(2 * g + 1).wait()
-        flat_ref = out_buf.at[g].reshape(devices * message, LANES)
-        for half in range(2):
-            for parity in range(BINS):
-                rows_ref = folded[half * BINS + parity]
-                for n in range(2):
-                    for i in range(2):
-                        shot = x_buf[2 * g + i, half * 2 + n]
-                        head, tail = shot[:, :HALF], shot[:, HALF:]
-                        hi, lo = split(head - tail if parity else head + tail)
-                        at = pl.ds((n * 2 + i) * channels, channels)
-                        rows_ref[at, :HALF] = hi
-                        rows_ref[at, HALF : 2 * HALF] = hi
-                        rows_ref[at, 2 * HALF :] = lo
-                at = slice(2 * parity * devices, 2 * (parity + 1) * devices)
+        for sh in range(SPREAD):
+            for i in range(2):
+                shot = x_buf[2 * g + i, sh]
+                head, tail = shot[:, :HALF], shot[:, HALF:]
+                at = pl.ds((sh * 2 + i) * channels, channels)
+                for rows_ref, rows in zip(folded, (head + tail, head - tail)):
+                    hi, lo = split(rows)
+                    rows_ref[at, :HALF] = hi
+                    rows_ref[at, HALF : 2 * HALF] = hi
+                    rows_ref[at, 2 * HALF :] = lo
+        for parity in range(BINS):
+            shot_rows = []
+            for half in range(2):
                 spectrum = lax.dot_general(
-                    table[at],
-                    rows_ref[...],
+                    table[parity * count : (parity + 1) * count],
+                    folded[parity][half * 2 * LANES : (half + 1) * 2 * LANES],
                     (((1,), (1,)), ((), ())),
                     preferred_element_type=jnp.float32,
                 )
                 for n in range(2):
-                    for part in range(2):
-                        row = parity * ROWS + 2 * (half * 2 + n) + part
-                        flat_ref[pl.ds(row, devices, stride=message), :] = spectrum[
-                            part * devices : (part + 1) * devices, n * LANES : (n + 1) * LANES
-                        ]
+                    shot_rows.append(
+                        spectrum[:, n * LANES : (n + 1) * LANES].reshape(-1, ROWS, LANES)
+                    )
+            a0, a2 = trade((shot_rows[0], shot_rows[2]), 4)
+            a1, a3 = trade((shot_rows[1], shot_rows[3]), 4)
+            devices = trade((a0, a1), 2) + trade((a2, a3), 2)
+            for n, rows in enumerate(devices):
+                out_buf[g, :, n, parity] = rows
         out_copy(g).start()
         return carry
 
@@ -113,17 +125,18 @@
     steps = shots // step
     table = jnp.asarray(dft_tables(radon_size, freq_size))
     any_space = pl.BlockSpec(memory_space=pl.ANY)
-    return pl.pallas_call(
+    groups = (devices // SPREAD, SPREAD, BINS)
+    out = pl.pallas_call(
         dft_kernel,
         in_specs=[any_space, any_space],
         out_specs=any_space,
-        out_shape=jax.ShapeDtypeStruct((devices, BINS, steps * ROWS, LANES), jnp.float32),
+        out_shape=jax.ShapeDtypeStruct(groups + (steps * ROWS, LANES), jnp.float32),
         scratch_shapes=[
             pltpu.VMEM((2 * steps, step // 2, channels, NT), jnp.float32),
             pltpu.VMEM(table.shape, table.dtype),
-            pltpu.VMEM((steps, devices, BINS, ROWS, LANES), jnp.float32),
+            pltpu.VMEM((steps,) + groups + (ROWS, LANES), jnp.float32),
         ]
-        + [pltpu.VMEM((4 * channels, 3 * HALF), jnp.bfloat16)] * (2 * BINS)
+        + [pltpu.VMEM((step * channels, 3 * HALF), jnp.bfloat16)] * BINS
         + [
             pltpu.SemaphoreType.DMA((2 * steps,)),
             pltpu.SemaphoreType.DMA,
@@ -136,6 +149,7 @@
             transcendentals=0,
         ),
     )(traces, table)
+    return out.reshape(devices, BINS, steps * ROWS, LANES)
 
 
 def weights_kernel(w_ref, out_ref):

time: 159 us -> 160 us (level)
  blocking collectives: 24.3 us -> 27.8 us
  waiting for transfers between devices: 80.8 us -> 78.8 us
    all_to_all x1, blocking collectives: 24.3 us -> 27.8 us  [shards(): result = lax.all_to_all(products, 'radon', 0, 0, tiled=True)]
    all_to_all x1, waiting for transfers between devices: 3.73 us -> 0.5 us  [shards(): received = lax.all_to_all(messages, ('radon', 'freq'), 0, 0, tiled=True)]
  transfers between devices with their start and end apart: 2 -> 2, of which waited for: 2 -> 2; matrix products, arithmetic and copies ran while one was open for 0% -> 0% of each run, Pallas kernels for 9% -> 8%
where the time goes in v5:
time: 160 us
  waiting for transfers between devices  78.8 us (49%)
  blocking collectives  27.8 us (17%)
  Pallas kernels  24.4 us (15%)
  between operations  13.5 us (8%)
  starting transfers between devices  11.9 us (7%)
  local copies, waits for them, and re-layouts  3.25 us (2%)
    all_gather x1, waiting for transfers between devices, shards(): weights = split_weights(lax.all_gather(radon_weights, 'freq', axis=0))  77.6 us
    all_to_all x1, blocking collectives, shards(): result = lax.all_to_all(products, 'radon', 0, 0, tiled=True)  27.8 us
    pallas_call x1, Pallas kernels, dft(): pl.pallas_call(dft_kernel, in_specs=[any_space, any_space], out_specs=any...  12.6 us
    all_to_all x1, starting transfers between devices, shards(): received = lax.all_to_all(messages, ('radon', 'freq'), 0, 0, tiled=True)  11.9 us
    pallas_call x1, Pallas kernels, panel_products(): pl.pallas_call(functools.partial(panel_kernel, count), grid=(grid,), in_s...  11.6 us
  transfers between devices with their start and end apart: 2, of which 2 were waited for; matrix products, arithmetic and copies ran while one was open for 0% of the time, Pallas kernels for 8%

profile of v5, /device:TPU:1, one launch (start us, length us, event | category | flops | bytes accessed | tf_op | source)
XLA Modules:
  0.0 159.7 jit_solution(17695327312069813417)
XLA Ops:
  6.5 0.0 all-gather.3.cloned.1.call-start
  6.5 0.7 all-gather.3.cloned.1.call-update
  7.3 12.6 %shard_map.64 = f32[32,4,2,48,128]{4,3,2,1,0:T(8,128)} custom-call(f32[48,64,1024]{2,1,0:T(8,128)} %x_hbm.1, bf16[512,1536]{1,0:T(8,128)(2,1)} %constant.4.clone.table_hbm), custom_call_target="tpu_custom_call" | custom-call | flops 4831838208 | bytes 18874368 | tf_op jit(solution)/shard_map/pallas_call | solution.py:129
  19.8 0.0 copy-start.1
  19.8 0.0 copy-start.3
  19.8 0.0 copy-start.2
  19.9 11.9 %all-to-all-start = ((f32[128,2,48,128]{3,2,1,0:T(8,128)}), f32[128,2,48,128]{3,2,1,0:T(8,128)}, u32[]{:S(2)}, u32[]{:S(2)}) async-start(f32[128,2,48,128]{3,2,1,0:T(8,128)} %bitcast.7), calls=%async_computation | async-start | bytes 12582912 | tf_op jit(solution)/shard_map/all_to_all | solution.py:291
  31.8 0.0 copy-done.1
  31.8 0.2 copy.11
  31.9 0.0 copy-done.3
  32.0 0.1 broadcast_in_dim.30
  32.1 0.1 broadcast_in_dim_reshape.4.refs_5_
  32.2 0.0 copy-done.2
  32.2 0.1 broadcast_in_dim.35.refs_7_
  32.3 0.1 broadcast_select_fusion
  32.4 77.6 %all-gather.3.cloned.1.call-done = f32[32,64,256]{2,1,0:T(8,128)} async-done(((f32[2,64,256]{2,1,0:T(8,128)}), f32[32,64,256]{2,1,0:T(8,128)}) %all-gather.3.cloned.1.call-update) | async-done | bytes 2097168 | tf_op jit(solution)/shard_map/all_gather | solution.py:289
  110.0 0.0 copy-start
  110.0 1.6 copy-done
  111.6 0.2 shard_map.65.refs_4_
  111.8 0.5 all-to-all-done.refs_0_.refs_1_.refs_2_.refs_3_
  112.3 11.6 %shard_map.66 = f32[8,2,2,48,256]{4,3,2,1,0:T(8,128)S(1)} custom-call(f32[128,2,48,128]{3,2,1,0:T(8,128)} %all-to-all-done.refs_0_.refs_1_.refs_2_.refs_3_, f32[128,2,48,128]{3,2,1,0:T(8,128)} %all-to-all-done.refs_0_.refs_1_.refs_2_.refs_3_, f32[128,2,48,128]{3,2,1,0:T(8,128)} %all-to-all-done.refs_0_.refs_1_.refs_2_.refs_3_, ...), custom_call_target="tpu_custom_call" | custom-call | flops 4831838208 | bytes 6291456 | tf_op jit(solution)/shard_map/pallas_call | solution.py:256
  123.9 27.8 %all_to_all.10 = f32[8,2,2,48,256]{4,3,2,1,0:T(8,128)S(1)} all-to-all(f32[8,2,2,48,256]{4,3,2,1,0:T(8,128)S(1)} %shard_map.66), channel_id=1, replica_groups=mesh['radon'=8,'freq'=16] {'radon'}, dimensions={0} | all-to-all | bytes 3145728 | tf_op jit(solution)/shard_map/all_to_all | solution.py:300
  151.7 1.1 copy.15
  (1 shorter events, 0.0 us)
Async XLA Ops:
  6.5 103.5 %all-gather.3.cloned.1.call-start = ((), (), s32[]{:S(2)}) async-start(), calls=%async_computation.2 | async-start | bytes 2228224 | tf_op jit(solution)/shard_map/all_gather | solution.py:289
  19.8 11.9 %copy-start.1 = (f32[384,256]{1,0:T(8,128)S(1)}, f32[384,256]{1,0:T(8,128)}, u32[]{:S(2)}) copy-start(f32[384,256]{1,0:T(8,128)} %param.8) | copy-start | bytes 1179652
  19.8 12.1 %copy-start.3 = (s32[384]{0:T(512)S(1)}, s32[384]{0:T(512)}, u32[]{:S(2)}) copy-start(s32[384]{0:T(512)} %param.9) | copy-start | bytes 4612
  19.8 12.4 %copy-start.2 = (s32[384]{0:T(512)S(1)}, s32[384]{0:T(512)}, u32[]{:S(2)}) copy-start(s32[384]{0:T(512)} %param.10) | copy-start | bytes 4612
  19.9 92.5 %all-to-all-start = ((f32[128,2,48,128]{3,2,1,0:T(8,128)}), f32[128,2,48,128]{3,2,1,0:T(8,128)}, u32[]{:S(2)}, u32[]{:S(2)}) async-start(f32[128,2,48,128]{3,2,1,0:T(8,128)} %bitcast.7), calls=%async_computation | async-start | bytes 12582912 | tf_op jit(solution)/shard_map/all_to_all | solution.py:291
  110.0 1.6 copy-start
Sparse Core Ops, SparseCore 0:
  9.8 100.1 all-gather.2

commit v6 on v5

--- a/solution.py
+++ b/solution.py
@@ -43,7 +43,7 @@
     table = (np.concatenate(rows) * NT ** (-0.5)).astype(np.float32)
     hi = table.astype(ml_dtypes.bfloat16)
     lo = (table - hi.astype(np.float32)).astype(ml_dtypes.bfloat16)
-    return np.concatenate([hi, lo, hi], axis=1)
+    return np.concatenate([hi, lo], axis=1)
 
 
 def trade(pieces, block):
@@ -56,35 +56,50 @@
     )
 
 
-def dft_kernel(x_hbm, table_hbm, out_hbm, x_buf, table, out_buf, *refs):
-    folded, (x_sems, table_sem, out_sems) = refs[:-3], refs[-3:]
+def dft_kernel(line_ref, x_hbm, table_hbm, out_hbm, x_buf, table, out_buf, *refs):
+    folded, (order, x_sems, table_sem, out_sems) = refs[:-4], refs[-4:]
     steps = out_buf.shape[0]
-    pieces, shots, channels, _ = x_buf.shape
+    shots, channels, _ = x_buf.shape
+    step = shots // steps
     count = table.shape[0] // BINS
 
-    table_copy = pltpu.make_async_copy(table_hbm, table, table_sem)
+    table_copy = pltpu.make_async_copy(table_hbm, table.at[:, : 2 * HALF], table_sem)
     table_copy.start()
 
+    offset = lax.axis_index("radon") * shots
+
+    def place(shot, counts):
+        line = line_ref[offset + shot]
+        order[jnp.where(line == 0, counts[0], counts[1])] = shot
+        return (counts[0] + (1 - line), counts[1] + line)
+
+    lax.fori_loop(0, shots, place, (jnp.int32(0), jnp.int32(shots // L)))
+
     def x_copy(n):
-        return pltpu.make_async_copy(
-            x_hbm.at[pl.ds(n * shots, shots)], x_buf.at[n], x_sems.at[n]
-        )
-
-    for n in range(pieces):
-        x_copy(n).start()
-    table_copy.wait()
+        return pltpu.make_async_copy(x_hbm.at[order[n]], x_buf.at[n], x_sems.at[n])
 
     def out_copy(g):
         return pltpu.make_async_copy(
             out_buf.at[g], out_hbm.at[:, :, :, pl.ds(g * ROWS, ROWS), :], out_sems.at[g]
         )
 
+    for n in range(2 * step):
+        x_copy(n).start()
+    table_copy.wait()
+    table[:, 2 * HALF :] = table[:, :HALF]
+
     def body(g, carry):
-        x_copy(2 * g).wait()
-        x_copy(2 * g + 1).wait()
+        for n in range(step):
+            x_copy(g * step + n).wait()
+
+        @pl.when(g + 2 < steps)
+        def _():
+            for n in range(step):
+                x_copy((g + 2) * step + n).start()
+
         for sh in range(SPREAD):
             for i in range(2):
-                shot = x_buf[2 * g + i, sh]
+                shot = x_buf[g * step + SPREAD * i + sh]
                 head, tail = shot[:, :HALF], shot[:, HALF:]
                 at = pl.ds((sh * 2 + i) * channels, channels)
                 for rows_ref, rows in zip(folded, (head + tail, head - tail)):
@@ -118,7 +133,7 @@
         out_copy(g).wait()
 
 
-def dft(traces, radon_size, freq_size):
+def dft(line_index, traces, radon_size, freq_size):
     shots, channels, _ = traces.shape
     devices = radon_size * freq_size
     step = LANES // channels * SPREAD
@@ -128,27 +143,28 @@
     groups = (devices // SPREAD, SPREAD, BINS)
     out = pl.pallas_call(
         dft_kernel,
-        in_specs=[any_space, any_space],
+        in_specs=[pl.BlockSpec(memory_space=pltpu.SMEM), any_space, any_space],
         out_specs=any_space,
         out_shape=jax.ShapeDtypeStruct(groups + (steps * ROWS, LANES), jnp.float32),
         scratch_shapes=[
-            pltpu.VMEM((2 * steps, step // 2, channels, NT), jnp.float32),
-            pltpu.VMEM(table.shape, table.dtype),
+            pltpu.VMEM(traces.shape, jnp.float32),
+            pltpu.VMEM((table.shape[0], 3 * HALF), table.dtype),
             pltpu.VMEM((steps,) + groups + (ROWS, LANES), jnp.float32),
         ]
         + [pltpu.VMEM((step * channels, 3 * HALF), jnp.bfloat16)] * BINS
         + [
-            pltpu.SemaphoreType.DMA((2 * steps,)),
+            pltpu.SMEM((shots,), jnp.int32),
+            pltpu.SemaphoreType.DMA((shots,)),
             pltpu.SemaphoreType.DMA,
             pltpu.SemaphoreType.DMA((steps,)),
         ],
         compiler_params=pltpu.CompilerParams(vmem_limit_bytes=60 * 2**20),
         cost_estimate=pl.CostEstimate(
-            flops=2 * table.size * shots * channels,
+            flops=3 * table.size * shots * channels,
             bytes_accessed=6 * traces.size,
             transcendentals=0,
         ),
-    )(traces, table)
+    )(line_index, traces, table)
     return out.reshape(devices, BINS, steps * ROWS, LANES)
 
 
@@ -178,38 +194,47 @@
 
 def panel_kernel(count, *refs):
     rec_refs, refs = refs[:count], refs[count:]
-    (w_ref, line_ref, src_ref, panel_ref, out_ref, a_hi, a_lo), gathers = refs[:7], refs[7:]
+    (w_ref, src_ref, panel_ref, back_ref, out_ref), refs = refs[:5], refs[5:]
+    a_refs, gathers = refs[: 2 * L], refs[2 * L :]
     step = pl.program_id(0)
     steps = pl.num_programs(0)
     freq_size, bins, height, _ = rec_refs[0].shape
     channels = w_ref.shape[1] // freq_size
-    tiles = height // ROWS
+    tiles = height // ROWS // L
+    halves = P_SIZE // LANES
 
     low = lax.broadcasted_iota(jnp.int32, (ROWS, LANES), 1) < channels
-    for parity in range(bins):
-        for r, rec_ref in enumerate(rec_refs):
-            for t in range(tiles):
-                firsts, seconds = [], []
-                for j in range(0, freq_size, 2):
-                    a = rec_ref[j, parity, pl.ds(t * ROWS, ROWS), :]
-                    b = rec_ref[j + 1, parity, pl.ds(t * ROWS, ROWS), :]
-                    firsts.append(jnp.where(low, a, pltpu.roll(b, channels, 1)))
-                    seconds.append(jnp.where(low, pltpu.roll(a, channels, 1), b))
-                both = jnp.concatenate(
-                    [jnp.concatenate(firsts, axis=1), jnp.concatenate(seconds, axis=1)], axis=0
-                )
-                at = pl.ds(((parity * count + r) * tiles + t) * 2 * ROWS, 2 * ROWS)
-                a_hi[at, :], a_lo[at, :] = split(both)
-    lines = dot3((a_hi[...], a_lo[...]), (w_ref[0], w_ref[1]))
-    rows = a_hi.shape[0] // bins
-    first_line = line_ref[...] == 0
-    for parity in range(bins):
-        own = lines[parity * rows : (parity + 1) * rows]
-        chosen = jnp.where(first_line, own[:, :P_SIZE], own[:, P_SIZE:])
-        for h in range(P_SIZE // LANES):
-            gathers[parity * (P_SIZE // LANES) + h][
-                pl.ds(pl.multiple_of(step * rows, rows), rows), :
-            ] = chosen[:, h * LANES : (h + 1) * LANES]
+    rows = tiles * 2 * ROWS
+    for line in range(L):
+        a_hi, a_lo = a_refs[2 * line : 2 * line + 2]
+        for parity in range(bins):
+            for r, rec_ref in enumerate(rec_refs):
+                for t in range(tiles):
+                    firsts, seconds = [], []
+                    for j in range(0, freq_size, 2):
+                        at = pl.ds((line * tiles + t) * ROWS, ROWS)
+                        a = rec_ref[j, parity, at, :]
+                        b = rec_ref[j + 1, parity, at, :]
+                        firsts.append(jnp.where(low, a, pltpu.roll(b, channels, 1)))
+                        seconds.append(jnp.where(low, pltpu.roll(a, channels, 1), b))
+                    both = jnp.concatenate(
+                        [jnp.concatenate(firsts, axis=1), jnp.concatenate(seconds, axis=1)],
+                        axis=0,
+                    )
+                    at = pl.ds((parity * count + r) * rows + t * 2 * ROWS, 2 * ROWS)
+                    a_hi[at, :], a_lo[at, :] = split(both)
+        weights = w_ref[0, :, line * P_SIZE : (line + 1) * P_SIZE], w_ref[
+            1, :, line * P_SIZE : (line + 1) * P_SIZE
+        ]
+        found = dot3((a_hi[...], a_lo[...]), weights)
+        for parity in range(bins):
+            for r in range(count):
+                start = pl.multiple_of(((step * count + r) * L + line) * rows, rows)
+                own = found[(parity * count + r) * rows : (parity * count + r + 1) * rows]
+                for h in range(halves):
+                    gathers[parity * halves + h][pl.ds(start, rows), :] = own[
+                        :, h * LANES : (h + 1) * LANES
+                    ]
 
     @pl.when(step == steps - 1)
     def _():
@@ -217,23 +242,39 @@
         own = shots // out_ref.shape[0]
         source = split(src_ref[...])
         first = panel_ref[...] == 0
+        blocks, block, _ = back_ref.shape
         for parity in range(bins):
             left, panels = ([], []), []
             for part in range(2):
                 at = pl.ds(part, shots, stride=2)
-                both = jnp.concatenate(
-                    [
-                        gathers[parity * (P_SIZE // LANES) + h][at, :]
-                        for h in range(P_SIZE // LANES)
-                    ],
+                sorted_rows = jnp.concatenate(
+                    split(
+                        jnp.concatenate(
+                            [gathers[parity * halves + h][at, :] for h in range(halves)], axis=1
+                        )
+                    ),
                     axis=1,
                 )
-                panels.append(split(dot3(source, split(both))))
+                natural = jnp.concatenate(
+                    [
+                        jnp.dot(
+                            back_ref[n],
+                            sorted_rows[n * block : (n + 1) * block],
+                            preferred_element_type=jnp.float32,
+                        )
+                        for n in range(blocks)
+                    ],
+                    axis=0,
+                )
+                pieces = natural[:, :P_SIZE], natural[:, P_SIZE:]
+                panels.append(
+                    split(dot3(source, [piece.astype(jnp.bfloat16) for piece in pieces]))
+                )
                 for k in range(K):
-                    hi, lo = split(jnp.where(first == (k == 0), both, 0.0))
-                    left[0].append(hi)
-                    left[1].append(lo)
-            left = [jnp.concatenate(pieces, axis=1) for pieces in left]
+                    for kept, piece in zip(left, pieces):
+                        chosen = jnp.where(first == (k == 0), piece, 0.0)
+                        kept.append(chosen.astype(jnp.bfloat16))
+            left = [jnp.concatenate(kept, axis=1) for kept in left]
             real, imag = panels
             rights = (
                 [jnp.concatenate([real[n], -imag[n]], axis=0) for n in range(2)],
@@ -245,7 +286,7 @@
                     out_ref[r, parity, part] = product[r * own : (r + 1) * own]
 
 
-def panel_products(received, weights, lines, sources, panel_rows, radon_size):
+def panel_products(received, weights, sources, panel_rows, back, radon_size):
     _, depth, columns = weights.shape
     freq_size = received.shape[0] // radon_size
     grid = 2
@@ -264,21 +305,32 @@
         ]
         + [
             pl.BlockSpec(weights.shape, lambda r: (0, 0, 0)),
-            pl.BlockSpec((rows, 1), lambda r: (r, 0)),
             pl.BlockSpec(sources.shape, lambda r: (0, 0)),
             pl.BlockSpec((shots, 1), lambda r: (0, 0)),
+            pl.BlockSpec(back.shape, lambda r: (0, 0, 0)),
         ],
         out_specs=pl.BlockSpec(out, lambda r: (0, 0, 0, 0, 0)),
         out_shape=jax.ShapeDtypeStruct(out, jnp.float32),
-        scratch_shapes=[pltpu.VMEM((BINS * rows, depth), jnp.bfloat16)] * 2
+        scratch_shapes=[pltpu.VMEM((BINS * rows // L, depth), jnp.bfloat16)] * (2 * L)
         + [pltpu.VMEM((grid * rows, LANES), jnp.float32)] * (BINS * P_SIZE // LANES),
         compiler_params=pltpu.CompilerParams(vmem_limit_bytes=48 * 2**20),
         cost_estimate=pl.CostEstimate(
-            flops=6 * grid * BINS * rows * depth * columns,
+            flops=6 * grid * BINS * rows * depth * P_SIZE,
             bytes_accessed=4 * received.size,
             transcendentals=0,
         ),
-    )(*[received] * count, weights, lines, sources, panel_rows)
+    )(*[received] * count, weights, sources, panel_rows, back)
+
+
+def back_to_order(line_index, radon_size, blocks):
+    lines = line_index.reshape(radon_size, -1)
+    own = lines.shape[1]
+    ranks = [jnp.cumsum((lines == line).astype(jnp.int32), axis=1) - 1 for line in range(L)]
+    place = jnp.where(lines == 0, ranks[0], ranks[1] + own // L)
+    place = place + own * (jnp.arange(radon_size, dtype=jnp.int32) % (radon_size // blocks))[:, None]
+    place = place.reshape(blocks, -1)
+    spots = jnp.arange(place.shape[1], dtype=jnp.int32)
+    return (place[:, :, None] == spots[None, None, :]).astype(jnp.bfloat16)
 
 
 def shards(shot_traces, radon_weights, source_weights, line_index, panel_index):
@@ -287,15 +339,15 @@
     radon_size = lax.axis_size("radon")
 
     weights = split_weights(lax.all_gather(radon_weights, "freq", axis=0))
-    messages = dft(shot_traces, radon_size, freq_size)
+    messages = dft(line_index, shot_traces, radon_size, freq_size)
     received = lax.all_to_all(messages, ("radon", "freq"), 0, 0, tiled=True)
 
-    lines = jnp.repeat(line_index, 2)[:, None]
     onehot = panel_index[None, :] == jnp.arange(K, dtype=jnp.int32)[:, None]
     sources = jnp.where(onehot[:, None, :], source_weights.T[None], 0.0).reshape(K * P_SIZE, -1)
 
+    back = back_to_order(line_index, radon_size, 2)
     products = panel_products(
-        received, weights, lines, sources, panel_index[:, None], radon_size
+        received, weights, sources, panel_index[:, None], back, radon_size
     )
     result = lax.all_to_all(products, "radon", 0, 0, tiled=True)
     return result.reshape(radon_size * BINS, 2, shot_rows, P_SIZE)

time: 160 us -> 159 us (level)
  Pallas kernels: 24.4 us -> 21.8 us
  transfers between devices with their start and end apart: 2 -> 2, of which waited for: 2 -> 1; matrix products, arithmetic and copies ran while one was open for 0% -> 1% of each run, Pallas kernels for 8% -> 7%
where the time goes in v6:
time: 159 us
  waiting for transfers between devices  78.7 us (49%)
  blocking collectives  28.4 us (18%)
  Pallas kernels  21.8 us (14%)
  between operations  13.5 us (8%)
  starting transfers between devices  11.9 us (7%)
  local copies, waits for them, and re-layouts  3.58 us (2%)
    all_gather x1, waiting for transfers between devices, shards(): weights = split_weights(lax.all_gather(radon_weights, 'freq', axis=0))  78 us
    all_to_all x1, blocking collectives, shards(): result = lax.all_to_all(products, 'radon', 0, 0, tiled=True)  28.4 us
    all_to_all x1, starting transfers between devices, shards(): received = lax.all_to_all(messages, ('radon', 'freq'), 0, 0, tiled=True)  11.9 us
    pallas_call x1, Pallas kernels, dft(): pl.pallas_call(dft_kernel, in_specs=[pl.BlockSpec(memory_space=pltpu.SMEM...  11.1 us
    pallas_call x1, Pallas kernels, panel_products(): pl.pallas_call(functools.partial(panel_kernel, count), grid=(grid,), in_s...  10.5 us
  transfers between devices with their start and end apart: 2, of which 1 were waited for; matrix products, arithmetic and copies ran while one was open for 1% of the time, Pallas kernels for 7%

profile of v6, /device:TPU:1, one launch (start us, length us, event | category | flops | bytes accessed | tf_op | source)
XLA Modules:
  0.0 158.5 jit_solution(7619485242436545271)
XLA Ops:
  6.5 0.7 all-gather.3.cloned.1.call-update
  7.3 11.1 %shard_map.64 = f32[32,4,2,48,128]{4,3,2,1,0:T(8,128)} custom-call(s32[384]{0:T(512)} %line_ref.1, f32[48,64,1024]{2,1,0:T(8,128)} %x_hbm.1, bf16[512,1024]{1,0:T(8,128)(2,1)} %constant.36.clone.table_hbm), custom_call_target="tpu_custom_call" | custom-call | flops 4831838208 | bytes 18874368 | tf_op jit(solution)/shard_map/pallas_call | solution.py:144
  18.3 0.0 copy-start.1
  18.4 0.0 copy-start.3
  18.4 11.9 %all-to-all-start = ((f32[128,2,48,128]{3,2,1,0:T(8,128)}), f32[128,2,48,128]{3,2,1,0:T(8,128)}, u32[]{:S(2)}, u32[]{:S(2)}) async-start(f32[128,2,48,128]{3,2,1,0:T(8,128)} %bitcast.7), calls=%async_computation | async-start | bytes 12582912 | tf_op jit(solution)/shard_map/all_to_all | solution.py:343
  30.3 0.2 copy.10
  30.5 0.1 broadcast_in_dim.33.refs_6_
  30.6 0.1 add.52
  30.7 0.1 add.53
  30.8 0.1 eq.52
  30.9 0.1 reshape.82
  30.9 0.2 reduce_window_sum.17
  31.2 0.1 sub.7
  31.2 0.1 reshape.83
  31.3 0.2 reduce_window_sum.18
  31.5 0.1 add.50
  31.6 0.1 fusion.refs_7_
  31.8 0.1 broadcast_select_fusion
  31.8 78.0 %all-gather.3.cloned.1.call-done = f32[32,64,256]{2,1,0:T(8,128)} async-done(((f32[2,64,256]{2,1,0:T(8,128)}), f32[32,64,256]{2,1,0:T(8,128)}) %all-gather.3.cloned.1.call-update) | async-done | bytes 2097168 | tf_op jit(solution)/shard_map/all_gather | solution.py:341
  109.8 1.6 %copy-done = f32[32,64,256]{2,1,0:T(8,128)S(1)} copy-done((f32[32,64,256]{2,1,0:T(8,128)S(1)}, f32[32,64,256]{2,1,0:T(8,128)}, u32[]{:S(2)}) %copy-start) | copy-done | bytes 2097176
  111.4 0.2 shard_map.65.refs_4_
  111.6 10.5 %shard_map.66 = f32[8,2,2,48,256]{4,3,2,1,0:T(8,128)S(1)} custom-call(f32[128,2,48,128]{3,2,1,0:T(8,128)} %all-to-all-done.refs_0_.refs_1_.refs_2_.refs_3_, f32[128,2,48,128]{3,2,1,0:T(8,128)} %all-to-all-done.refs_0_.refs_1_.refs_2_.refs_3_, f32[128,2,48,128]{3,2,1,0:T(8,128)} %all-to-all-done.refs_0_.refs_1_.refs_2_.refs_3_, ...), custom_call_target="tpu_custom_call" | custom-call | flops 2415919104 | bytes 6291456 | tf_op jit(solution)/shard_map/pallas_call | solution.py:297
  122.1 28.4 %all_to_all.10 = f32[8,2,2,48,256]{4,3,2,1,0:T(8,128)S(1)} all-to-all(f32[8,2,2,48,256]{4,3,2,1,0:T(8,128)S(1)} %shard_map.66), channel_id=1, replica_groups=mesh['radon'=8,'freq'=16] {'radon'}, dimensions={0} | all-to-all | bytes 3145728 | tf_op jit(solution)/shard_map/all_to_all | solution.py:352
  150.5 1.1 copy.13
  (13 shorter events, 0.1 us)
Async XLA Ops:
  6.5 103.3 %all-gather.3.cloned.1.call-start = ((), (), s32[]{:S(2)}) async-start(), calls=%async_computation.2 | async-start | bytes 2228224 | tf_op jit(solution)/shard_map/all_gather | solution.py:341
  18.3 12.0 %copy-start.1 = (f32[384,256]{1,0:T(8,128)S(1)}, f32[384,256]{1,0:T(8,128)}, u32[]{:S(2)}) copy-start(f32[384,256]{1,0:T(8,128)} %param.8) | copy-start | bytes 1179652
  18.3 12.1 %copy-start.2 = (s32[384]{0:T(512)S(1)}, s32[384]{0:T(512)}, u32[]{:S(2)}) copy-start(s32[384]{0:T(512)} %param.10) | copy-start | bytes 4612
  18.4 12.4 %copy-start.3 = (s32[384]{0:T(512)S(1)}, s32[384]{0:T(512)}, u32[]{:S(2)}) copy-start(s32[384]{0:T(512)} %line_ref.1) | copy-start | bytes 4612
  18.4 93.3 %all-to-all-start = ((f32[128,2,48,128]{3,2,1,0:T(8,128)}), f32[128,2,48,128]{3,2,1,0:T(8,128)}, u32[]{:S(2)}, u32[]{:S(2)}) async-start(f32[128,2,48,128]{3,2,1,0:T(8,128)} %bitcast.7), calls=%async_computation | async-start | bytes 12582912 | tf_op jit(solution)/shard_map/all_to_all | solution.py:343
  109.8 1.6 %copy-start = (f32[32,64,256]{2,1,0:T(8,128)S(1)}, f32[32,64,256]{2,1,0:T(8,128)}, u32[]{:S(2)}) copy-start(f32[32,64,256]{2,1,0:T(8,128)} %all-gather.3.cloned.1.call-done) | copy-start | bytes 6291460
Sparse Core Ops, SparseCore 0:
  9.8 99.9 all-gather.2

commit v7 on v6

--- a/solution.py
+++ b/solution.py
@@ -19,6 +19,7 @@
 BINS = 2
 ROWS = 8
 SPREAD = ROWS // 2
+AHEAD = 3
 
 
 def split(x):
@@ -83,7 +84,7 @@
             out_buf.at[g], out_hbm.at[:, :, :, pl.ds(g * ROWS, ROWS), :], out_sems.at[g]
         )
 
-    for n in range(2 * step):
+    for n in range(AHEAD * step):
         x_copy(n).start()
     table_copy.wait()
     table[:, 2 * HALF :] = table[:, :HALF]
@@ -92,10 +93,10 @@
         for n in range(step):
             x_copy(g * step + n).wait()
 
-        @pl.when(g + 2 < steps)
+        @pl.when(g + AHEAD < steps)
         def _():
             for n in range(step):
-                x_copy((g + 2) * step + n).start()
+                x_copy((g + AHEAD) * step + n).start()
 
         for sh in range(SPREAD):
             for i in range(2):
@@ -168,28 +169,38 @@
     return out.reshape(devices, BINS, steps * ROWS, LANES)
 
 
-def weights_kernel(w_ref, out_ref):
-    channels = w_ref.shape[2]
-    for j in range(w_ref.shape[0]):
+def weights_kernel(own_ref, other_ref, out_ref):
+    chips, _, channels, _ = own_ref.shape
+    even = lax.rem(lax.axis_index("freq"), 2) == 0
+    for chip in range(chips):
         for line in range(L):
-            at = (pl.ds(j * channels, channels), pl.ds(line * P_SIZE, P_SIZE))
-            hi, lo = split(w_ref[j, line])
-            out_ref[0, at[0], at[1]] = hi
-            out_ref[1, at[0], at[1]] = lo
-
-
-def split_weights(weights):
-    freq_size, _, channels, _ = weights.shape
+            own, other = own_ref[chip, line], other_ref[chip, line]
+            pair = jnp.where(even, own, other), jnp.where(even, other, own)
+            for core in range(2):
+                hi, lo = split(pair[core])
+                at = (
+                    pl.ds((2 * chip + core) * channels, channels),
+                    pl.ds(line * P_SIZE, P_SIZE),
+                )
+                out_ref[0, at[0], at[1]] = hi
+                out_ref[1, at[0], at[1]] = lo
+
+
+def all_weights(weights, freq_size):
+    groups = [list(range(core, freq_size, 2)) for core in range(2)]
+    own = lax.all_gather(weights, "freq", axis=0, axis_index_groups=groups)
+    other = lax.ppermute(own, "freq", [(j, j ^ 1) for j in range(freq_size)])
+    chips, _, channels, _ = own.shape
     return pl.pallas_call(
         weights_kernel,
         out_shape=jax.ShapeDtypeStruct(
-            (2, freq_size * channels, L * P_SIZE), jnp.bfloat16
+            (2, 2 * chips * channels, L * P_SIZE), jnp.bfloat16
         ),
         compiler_params=pltpu.CompilerParams(vmem_limit_bytes=32 * 2**20),
         cost_estimate=pl.CostEstimate(
-            flops=10**11, bytes_accessed=8 * weights.size, transcendentals=0
+            flops=10**11, bytes_accessed=16 * own.size, transcendentals=0
         ),
-    )(weights)
+    )(own, other)
 
 
 def panel_kernel(count, *refs):
@@ -338,7 +349,7 @@
     freq_size = lax.axis_size("freq")
     radon_size = lax.axis_size("radon")
 
-    weights = split_weights(lax.all_gather(radon_weights, "freq", axis=0))
+    weights = all_weights(radon_weights, freq_size)
     messages = dft(line_index, shot_traces, radon_size, freq_size)
     received = lax.all_to_all(messages, ("radon", "freq"), 0, 0, tiled=True)
 

time: 159 us -> 159 us (level)
  blocking collectives: 28.4 us -> 23.2 us
  local copies, waits for them, and re-layouts: 3.58 us -> 5.41 us
    all_to_all x1, blocking collectives: 28.4 us -> 23.2 us  [shards(): result = lax.all_to_all(products, 'radon', 0, 0, tiled=True)]
    ppermute x0 -> x1, waiting for transfers between devices: none -> 2.21 us  [all_weights(): other = lax.ppermute(own, 'freq', [(j, j ^ 1) for j in range(freq_size)])]
    unnamed x9 -> x13, local copies, waits for them, and re-layouts: 2.75 us -> 4.58 us
  transfers between devices with their start and end apart: 2 -> 3, of which waited for: 1 -> 2; matrix products, arithmetic and copies ran while one was open for 1% -> 1% of each run, Pallas kernels for 7% -> 7%
where the time goes in v7:
time: 159 us; the launch traced here: 157 us
  waiting for transfers between devices  80 us (50%)
  blocking collectives  23.2 us (15%)
  Pallas kernels  21.9 us (14%)
  between operations  13.5 us (8%)
  starting transfers between devices  12.4 us (8%)
  local copies, waits for them, and re-layouts  5.41 us (3%)
    all_gather x1, waiting for transfers between devices, all_weights(): own = lax.all_gather(weights, 'freq', axis=0, axis_index_groups=groups)  77.1 us
    all_to_all x1, blocking collectives, shards(): result = lax.all_to_all(products, 'radon', 0, 0, tiled=True)  23.2 us
    all_to_all x1, starting transfers between devices, shards(): received = lax.all_to_all(messages, ('radon', 'freq'), 0, 0, tiled=True)  11.9 us
    pallas_call x1, Pallas kernels, dft(): pl.pallas_call(dft_kernel, in_specs=[pl.BlockSpec(memory_space=pltpu.SMEM...  11.1 us
    pallas_call x1, Pallas kernels, panel_products(): pl.pallas_call(functools.partial(panel_kernel, count), grid=(grid,), in_s...  10.5 us
    unnamed x13, local copies, waits for them, and re-layouts  4.58 us
  transfers between devices with their start and end apart: 3, of which 2 were waited for; matrix products, arithmetic and copies ran while one was open for 1% of the time, Pallas kernels for 7%

profile of v7, /device:TPU:1, one launch (start us, length us, event | category | flops | bytes accessed | tf_op | source)
XLA Modules:
  0.0 157.0 jit_solution(15552837672048133817)
XLA Ops:
  6.5 0.7 all-gather.3.cloned.1.call-update
  7.3 11.1 %shard_map.64 = f32[32,4,2,48,128]{4,3,2,1,0:T(8,128)} custom-call(s32[384]{0:T(512)} %line_ref.1, f32[48,64,1024]{2,1,0:T(8,128)} %x_hbm.1, bf16[512,1024]{1,0:T(8,128)(2,1)} %constant.36.clone.table_hbm), custom_call_target="tpu_custom_call" | custom-call | flops 4831838208 | bytes 18874368 | tf_op jit(solution)/shard_map/pallas_call | solution.py:145
  18.4 11.9 %all-to-all-start = ((f32[128,2,48,128]{3,2,1,0:T(8,128)}), f32[128,2,48,128]{3,2,1,0:T(8,128)}, u32[]{:S(2)}, u32[]{:S(2)}) async-start(f32[128,2,48,128]{3,2,1,0:T(8,128)} %bitcast.8), calls=%async_computation | async-start | bytes 12582912 | tf_op jit(solution)/shard_map/all_to_all | solution.py:354
  30.3 0.2 copy.10
  30.5 0.1 broadcast_in_dim.33.refs_6_
  30.6 0.1 add.53
  30.8 0.1 eq.52
  30.8 0.1 reshape.82
  30.9 0.2 reduce_window_sum.17
  31.1 0.1 sub.7
  31.2 0.1 reshape.83
  31.3 0.2 reduce_window_sum.18
  31.5 77.1 %all-gather.3.cloned.1.call-done = f32[16,64,256]{2,1,0:T(8,128)} async-done(((f32[2,64,256]{2,1,0:T(8,128)}), f32[16,64,256]{2,1,0:T(8,128)}) %all-gather.3.cloned.1.call-update) | async-done | bytes 1048592 | tf_op jit(solution)/shard_map/all_gather | solution.py:191
  108.6 0.5 collective-permute-start
  109.0 0.1 add.50
  109.2 0.1 fusion.refs_7_
  109.3 2.2 %collective-permute-done.other_ref = f32[8,2,64,256]{3,2,1,0:T(8,128)S(1)} collective-permute-done((f32[8,2,64,256]{3,2,1,0:T(8,128)}, f32[8,2,64,256]{3,2,1,0:T(8,128)S(1)}, u32[]{:S(2)}, u32[]{:S(2)}) %collective-permute-start) | collective-permute-done | bytes 1048608 | tf_op jit(solution)/shard_map/ppermute | solution.py:192
  111.5 1.0 copy-done.1
  112.5 1.2 copy-done
  113.7 1.2 copy-done.2
  115.0 0.3 shard_map.65.refs_4_
  115.3 10.5 %shard_map.66 = f32[8,2,2,48,256]{4,3,2,1,0:T(8,128)S(1)} custom-call(f32[128,2,48,128]{3,2,1,0:T(8,128)} %all-to-all-done.refs_0_.refs_1_.refs_2_.refs_3_, f32[128,2,48,128]{3,2,1,0:T(8,128)} %all-to-all-done.refs_0_.refs_1_.refs_2_.refs_3_, f32[128,2,48,128]{3,2,1,0:T(8,128)} %all-to-all-done.refs_0_.refs_1_.refs_2_.refs_3_, ...), custom_call_target="tpu_custom_call" | custom-call | flops 2415919104 | bytes 6291456 | tf_op jit(solution)/shard_map/pallas_call | solution.py:308
  125.8 23.2 %all_to_all.10 = f32[8,2,2,48,256]{4,3,2,1,0:T(8,128)S(1)} all-to-all(f32[8,2,2,48,256]{4,3,2,1,0:T(8,128)S(1)} %shard_map.66), channel_id=1, replica_groups=mesh['radon'=8,'freq'=16] {'radon'}, dimensions={0} | all-to-all | bytes 3145728 | tf_op jit(solution)/shard_map/all_to_all | solution.py:363
  149.0 1.1 copy.13
  (19 shorter events, 0.2 us)
Async XLA Ops:
  6.5 102.1 %all-gather.3.cloned.1.call-start = ((), (), s32[]{:S(2)}) async-start(), calls=%async_computation.2 | async-start | bytes 1179648 | tf_op jit(solution)/shard_map/all_gather | solution.py:191
  18.3 11.9 %copy-start.3 = (f32[384,256]{1,0:T(8,128)S(1)}, f32[384,256]{1,0:T(8,128)}, u32[]{:S(2)}) copy-start(f32[384,256]{1,0:T(8,128)} %param.8) | copy-start | bytes 1179652
  18.3 12.1 %copy-start.4 = (s32[384]{0:T(512)S(1)}, s32[384]{0:T(512)}, u32[]{:S(2)}) copy-start(s32[384]{0:T(512)} %param.10) | copy-start | bytes 4612
  18.3 12.4 %copy-start.5 = (s32[384]{0:T(512)S(1)}, s32[384]{0:T(512)}, u32[]{:S(2)}) copy-start(s32[384]{0:T(512)} %line_ref.1) | copy-start | bytes 4612
  18.4 97.0 %all-to-all-start = ((f32[128,2,48,128]{3,2,1,0:T(8,128)}), f32[128,2,48,128]{3,2,1,0:T(8,128)}, u32[]{:S(2)}, u32[]{:S(2)}) async-start(f32[128,2,48,128]{3,2,1,0:T(8,128)} %bitcast.8), calls=%async_computation | async-start | bytes 12582912 | tf_op jit(solution)/shard_map/all_to_all | solution.py:354
  108.6 3.0 %collective-permute-start = (f32[8,2,64,256]{3,2,1,0:T(8,128)}, f32[8,2,64,256]{3,2,1,0:T(8,128)S(1)}, u32[]{:S(2)}, u32[]{:S(2)}) collective-permute-start(f32[8,2,64,256]{3,2,1,0:T(8,128)} %bitcast.6), channel_id=1, source_target_pairs={{0,1},{1,0},{2,3},{3,2},{4,5},{5,4},{6,7},{7,6},{8,9},{9,8},{10,11... | collective-permute-start | bytes 3145736 | tf_op jit(solution)/shard_map/ppermute | solution.py:192
  111.5 1.0 copy-start.1
  112.5 1.2 copy-start
  113.7 1.2 copy-start.2
Sparse Core Ops, SparseCore 0:
  9.7 98.8 all-gather.2

commit v8 on v6

--- a/solution.py
+++ b/solution.py
@@ -19,6 +19,8 @@
 BINS = 2
 ROWS = 8
 SPREAD = ROWS // 2
+AHEAD = 3
+GRID = 2
 
 
 def split(x):
@@ -32,9 +34,14 @@
     return dot(a[0], b[0]) + (dot(a[0], b[1]) + dot(a[1], b[0]))
 
 
+def exchange_order(radon_size, freq_size):
+    mixed = np.random.RandomState(7).permutation(radon_size // GRID * freq_size)
+    return mixed, np.concatenate([mixed + n * mixed.size for n in range(GRID)])
+
+
 def dft_tables(radon_size, freq_size):
     band = NF // freq_size
-    device = np.arange(radon_size * freq_size)
+    _, device = exchange_order(radon_size, freq_size)
     rows = []
     for parity in range(BINS):
         bins = band * (device % freq_size) + BINS * (device // freq_size) + parity
@@ -83,7 +90,7 @@
             out_buf.at[g], out_hbm.at[:, :, :, pl.ds(g * ROWS, ROWS), :], out_sems.at[g]
         )
 
-    for n in range(2 * step):
+    for n in range(AHEAD * step):
         x_copy(n).start()
     table_copy.wait()
     table[:, 2 * HALF :] = table[:, :HALF]
@@ -92,10 +99,10 @@
         for n in range(step):
             x_copy(g * step + n).wait()
 
-        @pl.when(g + 2 < steps)
+        @pl.when(g + AHEAD < steps)
         def _():
             for n in range(step):
-                x_copy((g + 2) * step + n).start()
+                x_copy((g + AHEAD) * step + n).start()
 
         for sh in range(SPREAD):
             for i in range(2):
@@ -192,13 +199,14 @@
     )(weights)
 
 
-def panel_kernel(count, *refs):
+def panel_kernel(spots, freq_size, *refs):
+    count = spots.size // freq_size
     rec_refs, refs = refs[:count], refs[count:]
     (w_ref, src_ref, panel_ref, back_ref, out_ref), refs = refs[:5], refs[5:]
     a_refs, gathers = refs[: 2 * L], refs[2 * L :]
     step = pl.program_id(0)
     steps = pl.num_programs(0)
-    freq_size, bins, height, _ = rec_refs[0].shape
+    _, bins, height, _ = rec_refs[0].shape
     channels = w_ref.shape[1] // freq_size
     tiles = height // ROWS // L
     halves = P_SIZE // LANES
@@ -208,13 +216,15 @@
     for line in range(L):
         a_hi, a_lo = a_refs[2 * line : 2 * line + 2]
         for parity in range(bins):
-            for r, rec_ref in enumerate(rec_refs):
+            for r in range(count):
                 for t in range(tiles):
                     firsts, seconds = [], []
                     for j in range(0, freq_size, 2):
                         at = pl.ds((line * tiles + t) * ROWS, ROWS)
-                        a = rec_ref[j, parity, at, :]
-                        b = rec_ref[j + 1, parity, at, :]
+                        a, b = (
+                            rec_refs[spot // freq_size][spot % freq_size, parity, at, :]
+                            for spot in spots[r * freq_size + j : r * freq_size + j + 2]
+                        )
                         firsts.append(jnp.where(low, a, pltpu.roll(b, channels, 1)))
                         seconds.append(jnp.where(low, pltpu.roll(a, channels, 1), b))
                     both = jnp.concatenate(
@@ -289,13 +299,14 @@
 def panel_products(received, weights, sources, panel_rows, back, radon_size):
     _, depth, columns = weights.shape
     freq_size = received.shape[0] // radon_size
-    grid = 2
+    grid = GRID
     count = radon_size // grid
+    spots = np.argsort(exchange_order(radon_size, freq_size)[0])
     shots = sources.shape[1]
     rows = shots // grid * 2
     out = (radon_size, BINS, 2, shots // radon_size, P_SIZE)
     return pl.pallas_call(
-        functools.partial(panel_kernel, count),
+        functools.partial(panel_kernel, spots, freq_size),
         grid=(grid,),
         in_specs=[
             pl.BlockSpec(
@@ -340,7 +351,10 @@
 
     weights = split_weights(lax.all_gather(radon_weights, "freq", axis=0))
     messages = dft(line_index, shot_traces, radon_size, freq_size)
-    received = lax.all_to_all(messages, ("radon", "freq"), 0, 0, tiled=True)
+    _, order = exchange_order(radon_size, freq_size)
+    received = lax.all_to_all(
+        messages, ("radon", "freq"), 0, 0, axis_index_groups=[order.tolist()], tiled=True
+    )
 
     onehot = panel_index[None, :] == jnp.arange(K, dtype=jnp.int32)[:, None]
     sources = jnp.where(onehot[:, None, :], source_weights.T[None], 0.0).reshape(K * P_SIZE, -1)

time: 159 us -> 169 us (1.063)
  waiting for transfers between devices: 78.7 us -> 86 us
    all_gather x1, waiting for transfers between devices: 78 us -> 85.3 us  [shards(): weights = split_weights(lax.all_gather(radon_weights, 'freq', axis=0))]
where the time goes in v8:
time: 169 us; the launch traced here: 167 us
  waiting for transfers between devices  86 us (51%)
  blocking collectives  29.5 us (17%)
  Pallas kernels  21.8 us (13%)
  between operations  13.5 us (8%)
  starting transfers between devices  11.9 us (7%)
  local copies, waits for them, and re-layouts  3.58 us (2%)
    all_gather x1, waiting for transfers between devices, shards(): weights = split_weights(lax.all_gather(radon_weights, 'freq', axis=0))  85.3 us
    all_to_all x1, blocking collectives, shards(): result = lax.all_to_all(products, 'radon', 0, 0, tiled=True)  29.5 us
    all_to_all x1, starting transfers between devices, shards(): lax.all_to_all(messages, ('radon', 'freq'), 0, 0, axis_index_groups=[orde...  11.9 us
    pallas_call x1, Pallas kernels, dft(): pl.pallas_call(dft_kernel, in_specs=[pl.BlockSpec(memory_space=pltpu.SMEM...  11.1 us
    pallas_call x1, Pallas kernels, panel_products(): pl.pallas_call(functools.partial(panel_kernel, spots, freq_size), grid=(g...  10.5 us
  transfers between devices with their start and end apart: 2, of which 1 were waited for; matrix products, arithmetic and copies ran while one was open for 1% of the time, Pallas kernels for 7%

profile of v8, /device:TPU:1, one launch (start us, length us, event | category | flops | bytes accessed | tf_op | source)
XLA Modules:
  0.0 166.9 jit_solution(17255122498722570899)
XLA Ops:
  6.5 0.7 all-gather.3.cloned.1.call-update
  7.3 11.1 %shard_map.64 = f32[32,4,2,48,128]{4,3,2,1,0:T(8,128)} custom-call(s32[384]{0:T(512)} %line_ref.1, f32[48,64,1024]{2,1,0:T(8,128)} %x_hbm.1, bf16[512,1024]{1,0:T(8,128)(2,1)} %constant.36.clone.table_hbm), custom_call_target="tpu_custom_call" | custom-call | flops 4831838208 | bytes 18874368 | tf_op jit(solution)/shard_map/pallas_call | solution.py:151
  18.3 0.0 copy-start.1
  18.3 0.0 copy-start.2
  18.4 11.9 %all-to-all-start = ((f32[128,2,48,128]{3,2,1,0:T(8,128)}), f32[128,2,48,128]{3,2,1,0:T(8,128)}, u32[]{:S(2)}, u32[]{:S(2)}) async-start(f32[128,2,48,128]{3,2,1,0:T(8,128)} %bitcast.7), calls=%async_computation | async-start | bytes 12582912 | tf_op jit(solution)/shard_map/all_to_all | solution.py:355
  30.3 0.2 copy.10
  30.5 0.1 broadcast_in_dim.33.refs_6_
  30.6 0.1 add.52
  30.7 0.1 add.53
  30.8 0.1 eq.52
  30.9 0.1 reshape.82
  30.9 0.2 reduce_window_sum.17
  31.1 0.1 sub.7
  31.2 0.1 reshape.83
  31.3 0.2 reduce_window_sum.18
  31.5 0.1 add.50
  31.6 0.1 fusion.refs_7_
  31.7 0.1 broadcast_select_fusion
  31.8 85.3 %all-gather.3.cloned.1.call-done = f32[32,64,256]{2,1,0:T(8,128)} async-done(((f32[2,64,256]{2,1,0:T(8,128)}), f32[32,64,256]{2,1,0:T(8,128)}) %all-gather.3.cloned.1.call-update) | async-done | bytes 2097168 | tf_op jit(solution)/shard_map/all_gather | solution.py:352
  117.1 1.6 copy-done
  118.7 0.2 shard_map.65.refs_4_
  118.9 10.5 %shard_map.66 = f32[8,2,2,48,256]{4,3,2,1,0:T(8,128)S(1)} custom-call(f32[128,2,48,128]{3,2,1,0:T(8,128)} %all-to-all-done.refs_0_.refs_1_.refs_2_.refs_3_, f32[128,2,48,128]{3,2,1,0:T(8,128)} %all-to-all-done.refs_0_.refs_1_.refs_2_.refs_3_, f32[128,2,48,128]{3,2,1,0:T(8,128)} %all-to-all-done.refs_0_.refs_1_.refs_2_.refs_3_, ...), custom_call_target="tpu_custom_call" | custom-call | flops 2415919104 | bytes 6291456 | tf_op jit(solution)/shard_map/pallas_call | solution.py:308
  129.4 29.5 %all_to_all.10 = f32[8,2,2,48,256]{4,3,2,1,0:T(8,128)S(1)} all-to-all(f32[8,2,2,48,256]{4,3,2,1,0:T(8,128)S(1)} %shard_map.66), channel_id=1, replica_groups=mesh['radon'=8,'freq'=16] {'radon'}, dimensions={0} | all-to-all | bytes 3145728 | tf_op jit(solution)/shard_map/all_to_all | solution.py:366
  158.9 1.1 copy.13
  (13 shorter events, 0.1 us)
Async XLA Ops:
  6.5 110.5 %all-gather.3.cloned.1.call-start = ((), (), s32[]{:S(2)}) async-start(), calls=%async_computation.2 | async-start | bytes 2228224 | tf_op jit(solution)/shard_map/all_gather | solution.py:352
  18.3 11.9 %copy-start.1 = (f32[384,256]{1,0:T(8,128)S(1)}, f32[384,256]{1,0:T(8,128)}, u32[]{:S(2)}) copy-start(f32[384,256]{1,0:T(8,128)} %param.8) | copy-start | bytes 1179652
  18.3 12.1 %copy-start.2 = (s32[384]{0:T(512)S(1)}, s32[384]{0:T(512)}, u32[]{:S(2)}) copy-start(s32[384]{0:T(512)} %param.10) | copy-start | bytes 4612
  18.4 12.4 %copy-start.3 = (s32[384]{0:T(512)S(1)}, s32[384]{0:T(512)}, u32[]{:S(2)}) copy-start(s32[384]{0:T(512)} %line_ref.1) | copy-start | bytes 4612
  18.4 100.5 %all-to-all-start = ((f32[128,2,48,128]{3,2,1,0:T(8,128)}), f32[128,2,48,128]{3,2,1,0:T(8,128)}, u32[]{:S(2)}, u32[]{:S(2)}) async-start(f32[128,2,48,128]{3,2,1,0:T(8,128)} %bitcast.7), calls=%async_computation | async-start | bytes 12582912 | tf_op jit(solution)/shard_map/all_to_all | solution.py:355
  117.1 1.6 copy-start
Sparse Core Ops, SparseCore 0:
  9.8 107.2 all-gather.2

commit v9 on v8

--- a/solution.py
+++ b/solution.py
@@ -35,13 +35,24 @@
 
 
 def exchange_order(radon_size, freq_size):
-    mixed = np.random.RandomState(7).permutation(radon_size // GRID * freq_size)
-    return mixed, np.concatenate([mixed + n * mixed.size for n in range(GRID)])
+    depth = radon_size // 2
+    sources = [depth * y_lo + z for z in range(depth) for y_lo in range(2)]
+    half = freq_size // 2
+    devices = [
+        (depth * y_lo + z) * freq_size + half * y_hi + n
+        for z in range(depth)
+        for y_hi in range(2)
+        for y_lo in range(2)
+        for n in range(half)
+    ]
+    count = radon_size // GRID
+    spots = [devices.index(r * freq_size + j) for r in sources[:count] for j in range(freq_size)]
+    return sources, spots, devices
 
 
 def dft_tables(radon_size, freq_size):
     band = NF // freq_size
-    _, device = exchange_order(radon_size, freq_size)
+    device = np.array(exchange_order(radon_size, freq_size)[2])
     rows = []
     for parity in range(BINS):
         bins = band * (device % freq_size) + BINS * (device // freq_size) + parity
@@ -199,8 +210,8 @@
     )(weights)
 
 
-def panel_kernel(spots, freq_size, *refs):
-    count = spots.size // freq_size
+def panel_kernel(order, spots, freq_size, *refs):
+    count = len(spots) // freq_size
     rec_refs, refs = refs[:count], refs[count:]
     (w_ref, src_ref, panel_ref, back_ref, out_ref), refs = refs[:5], refs[5:]
     a_refs, gathers = refs[: 2 * L], refs[2 * L :]
@@ -252,7 +263,6 @@
         own = shots // out_ref.shape[0]
         source = split(src_ref[...])
         first = panel_ref[...] == 0
-        blocks, block, _ = back_ref.shape
         for parity in range(bins):
             left, panels = ([], []), []
             for part in range(2):
@@ -265,17 +275,18 @@
                     ),
                     axis=1,
                 )
-                natural = jnp.concatenate(
-                    [
-                        jnp.dot(
-                            back_ref[n],
-                            sorted_rows[n * block : (n + 1) * block],
-                            preferred_element_type=jnp.float32,
-                        )
-                        for n in range(blocks)
-                    ],
-                    axis=0,
-                )
+                natural = [None] * len(order)
+                for n in range(0, len(order), count):
+                    mine = order[n : n + count]
+                    back = jnp.concatenate([back_ref[r * own : (r + 1) * own] for r in mine])
+                    found = jnp.dot(
+                        back,
+                        sorted_rows[n * own : (n + count) * own],
+                        preferred_element_type=jnp.float32,
+                    )
+                    for i, r in enumerate(mine):
+                        natural[r] = found[i * own : (i + 1) * own]
+                natural = jnp.concatenate(natural, axis=0)
                 pieces = natural[:, :P_SIZE], natural[:, P_SIZE:]
                 panels.append(
                     split(dot3(source, [piece.astype(jnp.bfloat16) for piece in pieces]))
@@ -301,12 +312,12 @@
     freq_size = received.shape[0] // radon_size
     grid = GRID
     count = radon_size // grid
-    spots = np.argsort(exchange_order(radon_size, freq_size)[0])
+    order, spots, _ = exchange_order(radon_size, freq_size)
     shots = sources.shape[1]
     rows = shots // grid * 2
     out = (radon_size, BINS, 2, shots // radon_size, P_SIZE)
     return pl.pallas_call(
-        functools.partial(panel_kernel, spots, freq_size),
+        functools.partial(panel_kernel, order, spots, freq_size),
         grid=(grid,),
         in_specs=[
             pl.BlockSpec(
@@ -318,7 +329,7 @@
             pl.BlockSpec(weights.shape, lambda r: (0, 0, 0)),
             pl.BlockSpec(sources.shape, lambda r: (0, 0)),
             pl.BlockSpec((shots, 1), lambda r: (0, 0)),
-            pl.BlockSpec(back.shape, lambda r: (0, 0, 0)),
+            pl.BlockSpec(back.shape, lambda r: (0, 0)),
         ],
         out_specs=pl.BlockSpec(out, lambda r: (0, 0, 0, 0, 0)),
         out_shape=jax.ShapeDtypeStruct(out, jnp.float32),
@@ -333,15 +344,16 @@
     )(*[received] * count, weights, sources, panel_rows, back)
 
 
-def back_to_order(line_index, radon_size, blocks):
+def back_to_order(line_index, order):
+    radon_size, count = len(order), len(order) // GRID
     lines = line_index.reshape(radon_size, -1)
     own = lines.shape[1]
     ranks = [jnp.cumsum((lines == line).astype(jnp.int32), axis=1) - 1 for line in range(L)]
     place = jnp.where(lines == 0, ranks[0], ranks[1] + own // L)
-    place = place + own * (jnp.arange(radon_size, dtype=jnp.int32) % (radon_size // blocks))[:, None]
-    place = place.reshape(blocks, -1)
-    spots = jnp.arange(place.shape[1], dtype=jnp.int32)
-    return (place[:, :, None] == spots[None, None, :]).astype(jnp.bfloat16)
+    offsets = np.array([own * (order.index(r) % count) for r in range(radon_size)], np.int32)
+    place = (place + offsets[:, None]).reshape(-1)
+    spots = jnp.arange(count * own, dtype=jnp.int32)
+    return (place[:, None] == spots[None, :]).astype(jnp.bfloat16)
 
 
 def shards(shot_traces, radon_weights, source_weights, line_index, panel_index):
@@ -351,15 +363,15 @@
 
     weights = split_weights(lax.all_gather(radon_weights, "freq", axis=0))
     messages = dft(line_index, shot_traces, radon_size, freq_size)
-    _, order = exchange_order(radon_size, freq_size)
+    order, _, places = exchange_order(radon_size, freq_size)
     received = lax.all_to_all(
-        messages, ("radon", "freq"), 0, 0, axis_index_groups=[order.tolist()], tiled=True
+        messages, ("radon", "freq"), 0, 0, axis_index_groups=[places], tiled=True
     )
 
     onehot = panel_index[None, :] == jnp.arange(K, dtype=jnp.int32)[:, None]
     sources = jnp.where(onehot[:, None, :], source_weights.T[None], 0.0).reshape(K * P_SIZE, -1)
 
-    back = back_to_order(line_index, radon_size, 2)
+    back = back_to_order(line_index, order)
     products = panel_products(
         received, weights, sources, panel_index[:, None], back, radon_size
     )

time: 169 us -> 152 us (0.90)
  waiting for transfers between devices: 86 us -> 77 us
  blocking collectives: 29.5 us -> 22.5 us
    all_gather x1, waiting for transfers between devices: 85.3 us -> 68.7 us  [shards(): weights = split_weights(lax.all_gather(radon_weights, 'freq', axis=0))]
    all_to_all x1, waiting for transfers between devices: 0.01 us -> 7.68 us  [shards(): lax.all_to_all(messages, ('radon', 'freq'), 0, 0, axis_index_groups=[plac...]
    all_to_all x1, blocking collectives: 29.5 us -> 22.5 us  [shards(): result = lax.all_to_all(products, 'radon', 0, 0, tiled=True)]
  transfers between devices with their start and end apart: 2 -> 2, of which waited for: 1 -> 2; matrix products, arithmetic and copies ran while one was open for 1% -> 1% of each run, Pallas kernels for 7% -> 7%
where the time goes in v9:
time: 152 us; the launch traced here: 151 us
  waiting for transfers between devices  77 us (51%)
  blocking collectives  22.5 us (15%)
  Pallas kernels  21.8 us (14%)
  between operations  13.5 us (9%)
  starting transfers between devices  11.9 us (8%)
  local copies, waits for them, and re-layouts  3.5 us (2%)
    all_gather x1, waiting for transfers between devices, shards(): weights = split_weights(lax.all_gather(radon_weights, 'freq', axis=0))  68.7 us
    all_to_all x1, blocking collectives, shards(): result = lax.all_to_all(products, 'radon', 0, 0, tiled=True)  22.5 us
    all_to_all x1, starting transfers between devices, shards(): lax.all_to_all(messages, ('radon', 'freq'), 0, 0, axis_index_groups=[plac...  11.9 us
    pallas_call x1, Pallas kernels, dft(): pl.pallas_call(dft_kernel, in_specs=[pl.BlockSpec(memory_space=pltpu.SMEM...  11.1 us
    pallas_call x1, Pallas kernels, panel_products(): pl.pallas_call(functools.partial(panel_kernel, order, spots, freq_size),...  10.5 us
    all_to_all x1, waiting for transfers between devices, shards(): lax.all_to_all(messages, ('radon', 'freq'), 0, 0, axis_index_groups=[plac...  7.68 us
  transfers between devices with their start and end apart: 2, of which 2 were waited for; matrix products, arithmetic and copies ran while one was open for 1% of the time, Pallas kernels for 7%

profile of v9, /device:TPU:1, one launch (start us, length us, event | category | flops | bytes accessed | tf_op | source)
XLA Modules:
  0.0 150.9 jit_solution(10572959972990783101)
XLA Ops:
  6.5 0.7 all-gather.3.cloned.1.call-update
  7.3 11.1 %shard_map.73 = f32[32,4,2,48,128]{4,3,2,1,0:T(8,128)} custom-call(s32[384]{0:T(512)} %line_ref.1, f32[48,64,1024]{2,1,0:T(8,128)} %x_hbm.1, bf16[512,1024]{1,0:T(8,128)(2,1)} %constant.20.clone.table_hbm), custom_call_target="tpu_custom_call" | custom-call | flops 4831838208 | bytes 18874368 | tf_op jit(solution)/shard_map/pallas_call | solution.py:162
  18.3 0.0 copy-start.2
  18.4 0.0 copy-start.4
  18.4 11.9 %all-to-all-start = ((f32[128,2,48,128]{3,2,1,0:T(8,128)}), f32[128,2,48,128]{3,2,1,0:T(8,128)}, u32[]{:S(2)}, u32[]{:S(2)}) async-start(f32[128,2,48,128]{3,2,1,0:T(8,128)} %bitcast.7), calls=%async_computation | async-start | bytes 12582912 | tf_op jit(solution)/shard_map/all_to_all | solution.py:367
  30.3 0.2 copy.11
  30.5 0.1 broadcast_in_dim.32.refs_6_
  30.6 0.1 add.37
  30.7 0.1 add.38
  30.8 0.1 reshape.59
  30.8 0.2 reduce_window_sum.17
  31.1 0.1 sub.7
  31.1 0.1 reshape.60
  31.2 0.2 reduce_window_sum.18
  31.4 0.1 add.35
  31.5 0.1 fusion.refs_7_
  31.7 0.1 broadcast_select_fusion
  31.7 68.7 %all-gather.3.cloned.1.call-done = f32[32,64,256]{2,1,0:T(8,128)} async-done(((f32[2,64,256]{2,1,0:T(8,128)}), f32[32,64,256]{2,1,0:T(8,128)}) %all-gather.3.cloned.1.call-update) | async-done | bytes 2097168 | tf_op jit(solution)/shard_map/all_gather | solution.py:364
  100.4 1.6 %copy-done = f32[32,64,256]{2,1,0:T(8,128)S(1)} copy-done((f32[32,64,256]{2,1,0:T(8,128)S(1)}, f32[32,64,256]{2,1,0:T(8,128)}, u32[]{:S(2)}) %copy-start) | copy-done | bytes 2097176
  102.0 0.2 shard_map.74.refs_4_
  102.2 7.7 %all-to-all-done.refs_0_.refs_1_.refs_2_.refs_3_ = f32[128,2,48,128]{3,2,1,0:T(8,128)} async-done(((f32[128,2,48,128]{3,2,1,0:T(8,128)}), f32[128,2,48,128]{3,2,1,0:T(8,128)}, u32[]{:S(2)}, u32[]{:S(2)}) %all-to-all-start) | async-done | bytes 6291488 | tf_op jit(solution)/shard_map/all_to_all | solution.py:367
  109.9 10.5 %shard_map.75 = f32[8,2,2,48,256]{4,3,2,1,0:T(8,128)S(1)} custom-call(f32[128,2,48,128]{3,2,1,0:T(8,128)} %all-to-all-done.refs_0_.refs_1_.refs_2_.refs_3_, f32[128,2,48,128]{3,2,1,0:T(8,128)} %all-to-all-done.refs_0_.refs_1_.refs_2_.refs_3_, f32[128,2,48,128]{3,2,1,0:T(8,128)} %all-to-all-done.refs_0_.refs_1_.refs_2_.refs_3_, ...), custom_call_target="tpu_custom_call" | custom-call | flops 2415919104 | bytes 6291456 | tf_op jit(solution)/shard_map/pallas_call | solution.py:319
  120.4 22.5 %all_to_all.10 = f32[8,2,2,48,256]{4,3,2,1,0:T(8,128)S(1)} all-to-all(f32[8,2,2,48,256]{4,3,2,1,0:T(8,128)S(1)} %shard_map.75), channel_id=1, replica_groups=mesh['radon'=8,'freq'=16] {'radon'}, dimensions={0} | all-to-all | bytes 3145728 | tf_op jit(solution)/shard_map/all_to_all | solution.py:378
  142.9 1.1 copy.14
  (13 shorter events, 0.1 us)
Async XLA Ops:
  6.5 93.9 %all-gather.3.cloned.1.call-start = ((), (), s32[]{:S(2)}) async-start(), calls=%async_computation.2 | async-start | bytes 2228224 | tf_op jit(solution)/shard_map/all_gather | solution.py:364
  18.3 12.0 %copy-start.1 = (f32[384,256]{1,0:T(8,128)S(1)}, f32[384,256]{1,0:T(8,128)}, u32[]{:S(2)}) copy-start(f32[384,256]{1,0:T(8,128)} %param.9) | copy-start | bytes 1179652
  18.3 12.1 %copy-start.2 = (s32[384]{0:T(512)S(1)}, s32[384]{0:T(512)}, u32[]{:S(2)}) copy-start(s32[384]{0:T(512)} %param.11) | copy-start | bytes 4612
  18.4 12.2 %copy-start.4 = (s32[8]{0:T(128)S(1)}, s32[8]{0:T(128)}, u32[]{:S(2)}) copy-start(s32[8]{0:T(128)} %constant.22) | copy-start | bytes 100
  18.4 12.4 %copy-start.3 = (s32[384]{0:T(512)S(1)}, s32[384]{0:T(512)}, u32[]{:S(2)}) copy-start(s32[384]{0:T(512)} %line_ref.1) | copy-start | bytes 4612
  18.4 91.5 %all-to-all-start = ((f32[128,2,48,128]{3,2,1,0:T(8,128)}), f32[128,2,48,128]{3,2,1,0:T(8,128)}, u32[]{:S(2)}, u32[]{:S(2)}) async-start(f32[128,2,48,128]{3,2,1,0:T(8,128)} %bitcast.7), calls=%async_computation | async-start | bytes 12582912 | tf_op jit(solution)/shard_map/all_to_all | solution.py:367
  100.4 1.6 %copy-start = (f32[32,64,256]{2,1,0:T(8,128)S(1)}, f32[32,64,256]{2,1,0:T(8,128)}, u32[]{:S(2)}) copy-start(f32[32,64,256]{2,1,0:T(8,128)} %all-gather.3.cloned.1.call-done) | copy-start | bytes 6291460
Sparse Core Ops, SparseCore 0:
  9.8 90.5 all-gather.2

commit v10 on v9

--- a/solution.py
+++ b/solution.py
@@ -52,10 +52,12 @@
 
 def dft_tables(radon_size, freq_size):
     band = NF // freq_size
-    device = np.array(exchange_order(radon_size, freq_size)[2])
+    order, _, places = exchange_order(radon_size, freq_size)
+    device = np.array(places)
+    first = band * (device % freq_size) + BINS * np.argsort(order)[device // freq_size]
     rows = []
     for parity in range(BINS):
-        bins = band * (device % freq_size) + BINS * (device // freq_size) + parity
+        bins = first + parity
         phase = (bins[:, None] * np.arange(HALF)[None, :] % NT) * (2.0 * np.pi / NT)
         rows.append(np.stack([np.cos(phase), -np.sin(phase)], axis=1).reshape(-1, HALF))
     table = (np.concatenate(rows) * NT ** (-0.5)).astype(np.float32)
@@ -303,8 +305,8 @@
             )
             for part in range(2):
                 product = dot3(left, rights[part])
-                for r in range(out_ref.shape[0]):
-                    out_ref[r, parity, part] = product[r * own : (r + 1) * own]
+                for n, r in enumerate(order):
+                    out_ref[n, parity, part] = product[r * own : (r + 1) * own]
 
 
 def panel_products(received, weights, sources, panel_rows, back, radon_size):
@@ -375,7 +377,7 @@
     products = panel_products(
         received, weights, sources, panel_index[:, None], back, radon_size
     )
-    result = lax.all_to_all(products, "radon", 0, 0, tiled=True)
+    result = lax.all_to_all(products, "radon", 0, 0, axis_index_groups=[order], tiled=True)
     return result.reshape(radon_size * BINS, 2, shot_rows, P_SIZE)
 
 

time: 152 us -> 152 us (level)
  no operation moved by 1% of the time
where the time goes in v10:
time: 152 us
  waiting for transfers between devices  77 us (51%)
  blocking collectives  23.1 us (15%)
  Pallas kernels  21.8 us (14%)
  between operations  13.5 us (9%)
  starting transfers between devices  11.9 us (8%)
  local copies, waits for them, and re-layouts  3.5 us (2%)
    all_gather x1, waiting for transfers between devices, shards(): weights = split_weights(lax.all_gather(radon_weights, 'freq', axis=0))  68.7 us
    all_to_all x1, blocking collectives, shards(): lax.all_to_all(products, 'radon', 0, 0, axis_index_groups=[order], tiled=...  23.1 us
    all_to_all x1, starting transfers between devices, shards(): lax.all_to_all(messages, ('radon', 'freq'), 0, 0, axis_index_groups=[plac...  11.9 us
    pallas_call x1, Pallas kernels, dft(): pl.pallas_call(dft_kernel, in_specs=[pl.BlockSpec(memory_space=pltpu.SMEM...  11.1 us
    pallas_call x1, Pallas kernels, panel_products(): pl.pallas_call(functools.partial(panel_kernel, order, spots, freq_size),...  10.5 us
    all_to_all x1, waiting for transfers between devices, shards(): lax.all_to_all(messages, ('radon', 'freq'), 0, 0, axis_index_groups=[plac...  7.68 us
  transfers between devices with their start and end apart: 2, of which 2 were waited for; matrix products, arithmetic and copies ran while one was open for 1% of the time, Pallas kernels for 7%

profile of v10, /device:TPU:1, one launch (start us, length us, event | category | flops | bytes accessed | tf_op | source)
XLA Modules:
  0.0 151.5 jit_solution(2420256412738026898)
XLA Ops:
  6.5 0.7 all-gather.3.cloned.1.call-update
  7.3 11.1 %shard_map.73 = f32[32,4,2,48,128]{4,3,2,1,0:T(8,128)} custom-call(s32[384]{0:T(512)} %line_ref.1, f32[48,64,1024]{2,1,0:T(8,128)} %x_hbm.1, bf16[512,1024]{1,0:T(8,128)(2,1)} %constant.20.clone.table_hbm), custom_call_target="tpu_custom_call" | custom-call | flops 4831838208 | bytes 18874368 | tf_op jit(solution)/shard_map/pallas_call | solution.py:164
  18.3 0.0 copy-start.2
  18.4 0.0 copy-start.4
  18.4 11.9 %all-to-all-start = ((f32[128,2,48,128]{3,2,1,0:T(8,128)}), f32[128,2,48,128]{3,2,1,0:T(8,128)}, u32[]{:S(2)}, u32[]{:S(2)}) async-start(f32[128,2,48,128]{3,2,1,0:T(8,128)} %bitcast.7), calls=%async_computation | async-start | bytes 12582912 | tf_op jit(solution)/shard_map/all_to_all | solution.py:369
  30.3 0.2 copy.11
  30.5 0.1 broadcast_in_dim.32.refs_6_
  30.6 0.1 add.37
  30.7 0.1 add.38
  30.8 0.1 reshape.59
  30.8 0.2 reduce_window_sum.17
  31.1 0.1 sub.7
  31.1 0.1 reshape.60
  31.2 0.2 reduce_window_sum.18
  31.4 0.1 add.35
  31.5 0.1 fusion.refs_7_
  31.7 0.1 broadcast_select_fusion
  31.7 68.7 %all-gather.3.cloned.1.call-done = f32[32,64,256]{2,1,0:T(8,128)} async-done(((f32[2,64,256]{2,1,0:T(8,128)}), f32[32,64,256]{2,1,0:T(8,128)}) %all-gather.3.cloned.1.call-update) | async-done | bytes 2097168 | tf_op jit(solution)/shard_map/all_gather | solution.py:366
  100.4 1.6 %copy-done = f32[32,64,256]{2,1,0:T(8,128)S(1)} copy-done((f32[32,64,256]{2,1,0:T(8,128)S(1)}, f32[32,64,256]{2,1,0:T(8,128)}, u32[]{:S(2)}) %copy-start) | copy-done | bytes 2097176
  102.0 0.2 shard_map.74.refs_4_
  102.2 7.7 %all-to-all-done.refs_0_.refs_1_.refs_2_.refs_3_ = f32[128,2,48,128]{3,2,1,0:T(8,128)} async-done(((f32[128,2,48,128]{3,2,1,0:T(8,128)}), f32[128,2,48,128]{3,2,1,0:T(8,128)}, u32[]{:S(2)}, u32[]{:S(2)}) %all-to-all-start) | async-done | bytes 6291488 | tf_op jit(solution)/shard_map/all_to_all | solution.py:369
  109.9 10.5 %shard_map.75 = f32[8,2,2,48,256]{4,3,2,1,0:T(8,128)S(1)} custom-call(f32[128,2,48,128]{3,2,1,0:T(8,128)} %all-to-all-done.refs_0_.refs_1_.refs_2_.refs_3_, f32[128,2,48,128]{3,2,1,0:T(8,128)} %all-to-all-done.refs_0_.refs_1_.refs_2_.refs_3_, f32[128,2,48,128]{3,2,1,0:T(8,128)} %all-to-all-done.refs_0_.refs_1_.refs_2_.refs_3_, ...), custom_call_target="tpu_custom_call" | custom-call | flops 2415919104 | bytes 6291456 | tf_op jit(solution)/shard_map/pallas_call | solution.py:321
  120.4 23.1 %all_to_all.10 = f32[8,2,2,48,256]{4,3,2,1,0:T(8,128)S(1)} all-to-all(f32[8,2,2,48,256]{4,3,2,1,0:T(8,128)S(1)} %shard_map.75), channel_id=1, replica_groups={{0,64,16,80,32,96,48,112},{1,65,17,81,33,97,49,113},{2,66,18,82,34,98,5..., dimensions={0} | all-to-all | bytes 3145728 | tf_op jit(solution)/shard_map/all_to_all | solution.py:380
  143.5 1.1 copy.14
  (13 shorter events, 0.1 us)
Async XLA Ops:
  6.5 93.9 %all-gather.3.cloned.1.call-start = ((), (), s32[]{:S(2)}) async-start(), calls=%async_computation.2 | async-start | bytes 2228224 | tf_op jit(solution)/shard_map/all_gather | solution.py:366
  18.3 12.0 %copy-start.1 = (f32[384,256]{1,0:T(8,128)S(1)}, f32[384,256]{1,0:T(8,128)}, u32[]{:S(2)}) copy-start(f32[384,256]{1,0:T(8,128)} %param.9) | copy-start | bytes 1179652
  18.3 12.1 %copy-start.2 = (s32[384]{0:T(512)S(1)}, s32[384]{0:T(512)}, u32[]{:S(2)}) copy-start(s32[384]{0:T(512)} %param.11) | copy-start | bytes 4612
  18.4 12.2 %copy-start.4 = (s32[8]{0:T(128)S(1)}, s32[8]{0:T(128)}, u32[]{:S(2)}) copy-start(s32[8]{0:T(128)} %constant.22) | copy-start | bytes 100
  18.4 12.4 %copy-start.3 = (s32[384]{0:T(512)S(1)}, s32[384]{0:T(512)}, u32[]{:S(2)}) copy-start(s32[384]{0:T(512)} %line_ref.1) | copy-start | bytes 4612
  18.4 91.5 %all-to-all-start = ((f32[128,2,48,128]{3,2,1,0:T(8,128)}), f32[128,2,48,128]{3,2,1,0:T(8,128)}, u32[]{:S(2)}, u32[]{:S(2)}) async-start(f32[128,2,48,128]{3,2,1,0:T(8,128)} %bitcast.7), calls=%async_computation | async-start | bytes 12582912 | tf_op jit(solution)/shard_map/all_to_all | solution.py:369
  100.4 1.6 %copy-start = (f32[32,64,256]{2,1,0:T(8,128)S(1)}, f32[32,64,256]{2,1,0:T(8,128)}, u32[]{:S(2)}) copy-start(f32[32,64,256]{2,1,0:T(8,128)} %all-gather.3.cloned.1.call-done) | copy-start | bytes 6291460
Sparse Core Ops, SparseCore 0:
  9.8 90.5 all-gather.2
